TPU v7x, 128 devices: a whole 4x4x4 slice. The times are simulated.
128 devices in a mesh: frame: 32 (over y, z, core), coil: 4 (over x).
Axes of the slice: x: 4, y: 4, z: 4, core: 2. Of those that a mesh axis runs over, the one named last changes fastest.
Arguments:
- spatial: float32 [8, 2, 320, 320], P(None, None, 'coil', 'frame'), may hold values from -6 to 6
- temporal: float32 [64, 8], P('frame'), may hold values from -2 to 2
- sensitivity: bfloat16 [8, 2, 320, 320], P('coil'), may hold values from -5 to 5
- coil_data: bfloat16 [64, 8, 2, 320, 320], P('frame', 'coil'), may hold values from -6 to 6
- kernel_index: int32 [64, 640, 640], P('frame'), may hold values from 0 to 7
- kernel_level: float32 [64, 8], P('frame'), may hold values from 0.02 to 4
Outputs:
- spatial_next: float32 [8, 2, 320, 320], P(None, None, 'coil', 'frame')
- images: bfloat16 [64, 2, 320, 320], P('frame')
All inputs are finite; a program needn't handle non-finite values.
Results may differ from a plain program's by a relative error of at most 0.001.
Values may be sent and summed in bfloat16 or wider, within the bound.
A program may use at most 128 MiB of HBM per device.

v0:
```python
import functools
import math

import jax
import jax.numpy as jnp
import ml_dtypes
import numpy as np
from jax import lax
from jax.experimental import pallas as pl
from jax.experimental.pallas import tpu as pltpu
from jax.sharding import PartitionSpec as P

STEP_SIZE = 0.15
BF = jnp.bfloat16
F32 = jnp.float32


def halves(table):
    high = table.astype(ml_dtypes.bfloat16)
    low = (table - high.astype(np.float64)).astype(ml_dtypes.bfloat16)
    return high, low


def make_tables(size):
    half = size // 2
    slots = -(-(size + 1) // 128) * 128
    rows = -(-(size + 1) // 16) * 16
    p = np.arange(half) + 0.5
    k = np.arange(slots)
    valid = (k <= size).astype(np.float64)
    angle = np.pi / size * np.outer(p, k)
    cos, sin = np.cos(angle) * valid, np.sin(angle) * valid
    cos[:, size] = 0.0
    sin[:, 0] = 0.0
    weight = np.where((k == 0) | (k == size), 0.5, 1.0)
    out = {}
    for name, tab in (("c", cos), ("s", sin)):
        hi, lo = halves(tab)
        out["f1" + name] = np.concatenate([hi, lo], axis=1)
        rhi, rlo = hi[:, :rows].T, lo[:, :rows].T
        out["f2" + name] = np.concatenate([rhi, rhi, rlo], axis=1)
        whi, wlo = halves(tab * weight)
        out["i1" + name] = np.concatenate([whi[:, :rows], whi[:, :rows], wlo[:, :rows]], axis=1)
        parts = []
        for j in range(0, slots, 128):
            parts += [whi.T[j:j + 128], whi.T[j:j + 128], wlo.T[j:j + 128]]
        out["i2" + name] = np.concatenate(parts, axis=0)
    wide = -(-half // 128) * 128
    place = np.zeros((size, 2 * wide))
    q = np.arange(half)
    place[half + q, q] = 1
    place[half - 1 - q, wide + q] = 1
    out["place"] = place.astype(ml_dtypes.bfloat16)
    out["unplace"] = place.T.astype(ml_dtypes.bfloat16)
    out["flip"] = np.eye(half)[::-1].astype(ml_dtypes.bfloat16)
    mirror = np.zeros((2 * size, slots))
    kk = np.arange(size + 1)
    mirror[(2 * size - kk) % (2 * size), kk] = 1
    out["mirror"] = mirror.astype(ml_dtypes.bfloat16)
    out["mirror_rows"] = mirror.T[:rows].astype(ml_dtypes.bfloat16)
    return out


TABLES = ("f1c", "f1s", "f2c", "f2s", "i1c", "i1s", "i2c", "i2s", "place", "unplace", "flip", "mirror", "mirror_rows")


def mm(a, b):
    return jnp.dot(a, b, preferred_element_type=F32)


def split(x):
    high = x.astype(BF)
    low = (x - high.astype(F32)).astype(BF)
    return high, low


def normal_kernel(level, image, sens, data, index, f1c, f1s, f2c, f2s, i1c, i1s, i2c, i2s, place, unplace, flip, mirror, mirror_rows, out, kq, sf, imf, res, lc, ls, ge, go, spa, spb, za, zb, lhc, lhs, oc, osn):
    frames, coils = image.shape[0], sens.shape[0]
    size = image.shape[2]
    half = size // 2
    wide = place.shape[1] // 2
    rows = f2c.shape[0]
    slots = mirror.shape[1]
    chunks = slots // 128
    levels = level.shape[1]

    for t in range(frames):
        ib = index[t].astype(F32).astype(BF)
        flipped = mm(ib, mirror[...]).astype(BF)
        low = mm(mirror_rows[...], jnp.concatenate([ib[:, :slots], flipped], axis=1))
        quads = (ib[:rows, :slots].astype(F32), flipped[:rows].astype(F32), low[:, :slots], low[:, slots:])
        for n, quad in enumerate(quads):
            value = jnp.full(quad.shape, level[t, 0], F32)
            for m in range(1, levels):
                value = jnp.where(quad > m - 0.5, level[t, m], value)
            kq[t, n] = value

    def folded(x):
        left = mm(flip[...], x[:half]).astype(BF)
        return mm(jnp.concatenate([x[half:], left], axis=0), place[...])

    for c in range(coils):
        for h in range(2):
            sf[c, h] = folded(sens[c, h])
    for t in range(frames):
        for h in range(2):
            imf[t, h] = folded(image[t, h])
    for t in range(frames):
        for c in range(coils):
            dr, di = folded(data[t, c, 0]), folded(data[t, c, 1])
            sr, si = sf[c, 0], sf[c, 1]
            gr, gi = -(sr * dr + si * di), si * dr - sr * di
            if c:
                gr, gi = res[t, 0] + gr, res[t, 1] + gi
            res[t, 0] = gr
            res[t, 1] = gi

    def pair(q, carry):
        t, c = q // coils, q % coils
        for r in range(0, half, 16):
            parts = {}
            for a, row in (("R", r), ("L", half + r)):
                for b, col in (("R", 0), ("L", wide)):
                    sl = (pl.ds(row, 16), pl.ds(col, half))
                    sr, si = sf[c, 0, sl[0], sl[1]], sf[c, 1, sl[0], sl[1]]
                    ir, ii = imf[t, 0, sl[0], sl[1]], imf[t, 1, sl[0], sl[1]]
                    parts[a + b] = (sr * ir - si * ii, sr * ii + si * ir)
            for h in range(2):
                rr, rl, lr, ll = (parts[n][h] for n in ("RR", "RL", "LR", "LL"))
                re, ro, le, lo = rr + rl, rr - rl, lr + ll, lr - ll
                for k, (xc, xs) in enumerate(((re + le, ro + lo), (re - le, ro - lo))):
                    at = (2 * k + h) * half + r
                    hc, wc = split(xc)
                    hs, ws = split(xs)
                    lc[0, pl.ds(at, 16)] = hc
                    lc[1, pl.ds(at, 16)] = wc
                    ls[0, pl.ds(at, 16)] = hs
                    ls[1, pl.ds(at, 16)] = ws
        for n, (lref, tab) in enumerate(((lc, f1c), (ls, f1s))):
            first = mm(lref[0], tab[:, :slots]) + mm(lref[0], tab[:, slots:]) + mm(lref[1], tab[:, :slots])
            for k, dest in enumerate((ge, go)):
                for h in range(2):
                    part = first[(2 * k + h) * half:(2 * k + h + 1) * half]
                    high, low = split(part)
                    for j in range(chunks):
                        lanes = pl.ds((2 * n + h) * 128, 128)
                        dest[j, pl.ds(0, half), lanes] = high[:, j * 128:(j + 1) * 128]
                        dest[j, pl.ds(half, half), lanes] = low[:, j * 128:(j + 1) * 128]
                        dest[j, pl.ds(2 * half, half), lanes] = high[:, j * 128:(j + 1) * 128]
        for j in range(chunks):
            spa[j] = mm(f2c[...], ge[j])
            spb[j] = mm(f2s[...], go[j])
            for r in range(0, rows, 16):
                rs = pl.ds(r, 16)
                aar, aai, abr, abi = (spa[j, rs, pl.ds(128 * m, 128)] for m in range(4))
                bar, bai, bbr, bbi = (spb[j, rs, pl.ds(128 * m, 128)] for m in range(4))
                kpp, kpm, kmp, kmm = (kq[t, m, rs, pl.ds(128 * j, 128)] for m in range(4))
                ur, ui, vr, vi = aar - bbr, aai - bbi, aar + bbr, aai + bbi
                wr, wi, qr, qi = abr + bar, abi + bai, abr - bar, abi - bai
                ppr, ppi = kpp * (ur + wi), kpp * (ui - wr)
                mmr, mmi = kmm * (ur - wi), kmm * (ui + wr)
                pmr, pmi = kpm * (vr - qi), kpm * (vi + qr)
                mpr, mpi = kmp * (vr + qi), kmp * (vi - qr)
                s1r, s1i, s2r, s2i = ppr + mmr, ppi + mmi, pmr + mpr, pmi + mpi
                d1r, d1i, d2r, d2i = ppr - mmr, ppi - mmi, pmr - mpr, pmi - mpi
                for dest, vals in ((za, (s1r + s2r, s1i + s2i, d2i - d1i, d1r - d2r)), (zb, (-(d1i + d2i), d1r + d2r, s2r - s1r, s2i - s1i))):
                    for m, value in enumerate(vals):
                        high, low = split(value)
                        lanes = pl.ds(128 * m, 128)
                        dest[j, pl.ds(r, 16), lanes] = high
                        dest[j, pl.ds(rows + r, 16), lanes] = low
                        dest[j, pl.ds(2 * rows + r, 16), lanes] = high
            for n, (tab, src) in enumerate(((i1c, za), (i1s, zb))):
                high, low = split(mm(tab[...], src[j]))
                for m in range(4):
                    dest = lhc if m < 2 else lhs
                    rs = pl.ds((2 * n + m % 2) * half, half)
                    for place_at, value in enumerate((high, low, high)):
                        dest[rs, pl.ds(j * 384 + place_at * 128, 128)] = value[:, 128 * m:128 * (m + 1)]
        oc[...] = mm(lhc[...], i2c[...])
        osn[...] = mm(lhs[...], i2s[...])
        for r in range(0, half, 16):
            quad = {}
            for h in range(2):
                ee, oe = oc[pl.ds(h * half + r, 16)], oc[pl.ds((2 + h) * half + r, 16)]
                eo, oo = osn[pl.ds(h * half + r, 16)], osn[pl.ds((2 + h) * half + r, 16)]
                quad["RR", h] = (ee + oe) + (eo + oo)
                quad["RL", h] = (ee + oe) - (eo + oo)
                quad["LR", h] = (ee - oe) + (eo - oo)
                quad["LL", h] = (ee - oe) - (eo - oo)
            for a, row in (("R", r), ("L", half + r)):
                for b, col in (("R", 0), ("L", wide)):
                    sl = (pl.ds(row, 16), pl.ds(col, half))
                    sr, si = sf[c, 0, sl[0], sl[1]], sf[c, 1, sl[0], sl[1]]
                    yr, yi = quad[a + b, 0], quad[a + b, 1]
                    res[t, 0, sl[0], sl[1]] += sr * yr + si * yi
                    res[t, 1, sl[0], sl[1]] += sr * yi - si * yr
        return carry

    lax.fori_loop(0, frames * coils, pair, 0)

    for t in range(frames):
        for h in range(2):
            high, low = split(res[t, h])
            cols = mm(high, unplace[...]) + mm(low, unplace[...])
            out[t, h, pl.ds(half, half)] = cols[:half]
            high, low = split(cols[half:])
            out[t, h, pl.ds(0, half)] = mm(flip[...], high) + mm(flip[...], low)


def partial_residual(images, sensitivity, coil_data, kernel_index, kernel_level):
    frames, _, size, _ = images.shape
    tables = make_tables(size)
    half = size // 2
    wide = tables["place"].shape[1] // 2
    rows = tables["f2c"].shape[0]
    slots = tables["mirror"].shape[1]
    chunks = slots // 128
    coils = sensitivity.shape[0]
    level = kernel_level / (4.0 * size * size)
    vm = pl.BlockSpec(memory_space=pltpu.VMEM)
    return pl.pallas_call(
        normal_kernel,
        out_shape=jax.ShapeDtypeStruct((frames, 2, size, size), F32),
        in_specs=[pl.BlockSpec(memory_space=pltpu.SMEM)] + [vm] * (4 + len(TABLES)),
        out_specs=vm,
        scratch_shapes=[
            pltpu.VMEM((frames, 4, rows, slots), F32),
            pltpu.VMEM((coils, 2, size, 2 * wide), F32),
            pltpu.VMEM((frames, 2, size, 2 * wide), F32),
            pltpu.VMEM((frames, 2, size, 2 * wide), F32),
            pltpu.VMEM((2, 4 * half, half), BF),
            pltpu.VMEM((2, 4 * half, half), BF),
            pltpu.VMEM((chunks, 3 * half, 512), BF),
            pltpu.VMEM((chunks, 3 * half, 512), BF),
            pltpu.VMEM((chunks, rows, 512), F32),
            pltpu.VMEM((chunks, rows, 512), F32),
            pltpu.VMEM((chunks, 3 * rows, 512), BF),
            pltpu.VMEM((chunks, 3 * rows, 512), BF),
            pltpu.VMEM((4 * half, 3 * slots), BF),
            pltpu.VMEM((4 * half, 3 * slots), BF),
            pltpu.VMEM((4 * half, half), F32),
            pltpu.VMEM((4 * half, half), F32),
        ],
        compiler_params=pltpu.CompilerParams(vmem_limit_bytes=60 * 2**20),
    )(level, images, sensitivity, coil_data, kernel_index, *[jnp.asarray(tables[n]) for n in TABLES])


def build_images(factors, temporal):
    mixed = jnp.einsum(
        "tr,rcxy->tcxy",
        temporal,
        lax.all_gather(factors, "frame", axis=3, tiled=True),
        precision=lax.Precision.HIGHEST,
    )
    row_images = mixed.astype(jnp.bfloat16)
    return lax.all_gather(row_images, "coil", axis=2, tiled=True)


def body(spatial, temporal, sensitivity, coil_data, kernel_index, kernel_level):
    full_images = build_images(spatial, temporal)
    partial_value = partial_residual(full_images, sensitivity, coil_data, kernel_index, kernel_level)
    rows_residual = lax.psum_scatter(partial_value, "coil", scatter_dimension=2, tiled=True)
    local_grad = jnp.einsum(
        "tr,tcxy->rcxy", temporal, rows_residual, precision=lax.Precision.HIGHEST
    )
    gradient = lax.psum_scatter(local_grad, "frame", scatter_dimension=3, tiled=True)
    spatial_next = spatial - STEP_SIZE * gradient
    images = build_images(spatial_next, temporal)
    return (spatial_next, images)


def solution(mesh):
    placed = (
        P(None, None, "coil", "frame"),
        P("frame", None),
        P("coil", None, None, None),
        P("frame", "coil", None, None, None),
        P("frame", None, None),
        P("frame", None),
    )
    return jax.shard_map(
        body,
        mesh=mesh,
        in_specs=placed,
        out_specs=(P(None, None, "coil", "frame"), P("frame", None, None, None)),
        check_vma=False,
    )
```

profile of v0, /device:TPU:1, one launch (start us, length us, event | category | flops | bytes accessed | tf_op | source)
XLA Modules:
  0.0 305.8 jit_solution(16051572770510936112)
XLA Ops:
  7.2 0.0 copy-start
  7.2 0.0 all-gather.3.cloned.1.call-start
  7.2 0.7 all-gather.3.cloned.1.call-update
  7.9 0.0 reduce-scatter.3.cloned.1.call-start
  8.0 1.2 broadcast_multiply_fusion.level
  9.2 49.5 %all-gather.3.cloned.1.call-done = f32[8,2,80,320]{2,1,3,0:T(2,128)} async-done(((f32[8,2,80,10]{2,1,3,0:T(2,128)}), f32[8,2,80,320]{2,1,3,0:T(2,128)}) %all-gather.3.cloned.1.call-update) | async-done | bytes 1638416 | tf_op jit(solution)/shard_map/all_gather | solution.py:253
  58.7 3.0 copy.32
  61.8 0.0 copy-done
  61.8 1.8 fusion.4
  63.6 13.3 %all_gather.13.image = bf16[2,2,320,320]{3,2,1,0:T(8,128)(2,1)} all-gather(bf16[2,2,80,320]{3,2,1,0:T(8,128)(2,1)S(1)} %copy.38), channel_id=1, replica_groups=mesh['frame'=32,'coil'=4] {'coil'}, dimensions={2}, use_global_device_ids=true | all-gather | bytes 1024000 | tf_op jit(solution)/shard_map/all_gather | solution.py:257
  76.8 42.9 %shard_map.194 = f32[2,2,320,320]{3,2,1,0:T(8,128)} custom-call(f32[2,8]{1,0:T(2,128)} %broadcast_multiply_fusion.level, bf16[2,2,320,320]{3,2,1,0:T(8,128)(2,1)} %all_gather.13.image, bf16[2,2,320,320]{3,2,1,0:T(8,128)(2,1)} %sens.1, bf16[2,2,2,320,320]{4,3,2,1,0:T(8,128)(2,1)} %data.1, s32[2,640,640]{2,1,0:T(8,128)} %index.1, ...), custom_call_target="tpu_custom_call" | custom-call | tf_op jit(solution)/shard_map/pallas_call | solution.py:222
  119.7 0.0 reduce-scatter.3.cloned.1.call-update
  119.8 0.0 reduce-scatter.5.cloned.1.call-start
  119.8 29.6 %reduce-scatter.3.cloned.1.call-done = f32[2,2,80,320]{3,2,1,0:T(8,128)} async-done(((f32[2,2,320,320]{3,2,1,0:T(8,128)}), f32[2,2,80,320]{3,2,1,0:T(8,128)}) %reduce-scatter.3.cloned.1.call-update) | async-done | bytes 409616 | tf_op jit(solution)/shard_map/reduce_scatter | solution.py:263
  149.4 3.1 convolution_bitcast_fusion
  152.5 2.2 copy.26
  154.6 0.0 copy-start.1
  154.6 0.0 reduce-scatter.5.cloned.1.call-update
  154.7 0.0 all-gather.5.cloned.1.call-start
  154.7 77.8 %reduce-scatter.5.cloned.1.call-done = f32[8,2,80,10]{2,0,1,3:T(8,128)} async-done(((f32[8,2,80,320]{2,0,1,3:T(8,128)}), f32[8,2,80,10]{2,0,1,3:T(8,128)}) %reduce-scatter.5.cloned.1.call-update) | async-done | bytes 51216 | tf_op jit(solution)/shard_map/reduce_scatter | solution.py:267
  232.5 0.0 copy-done.1
  232.5 1.5 copy_subtract_fusion
  234.0 0.0 all-gather.5.cloned.1.call-update
  234.0 1.6 copy.29
  235.6 45.7 %all-gather.5.cloned.1.call-done = f32[8,2,80,320]{2,0,1,3:T(8,128)} async-done(((f32[8,2,80,10]{2,0,1,3:T(8,128)}), f32[8,2,80,320]{2,0,1,3:T(8,128)}) %all-gather.5.cloned.1.call-update) | async-done | bytes 1638416 | tf_op jit(solution)/shard_map/all_gather | solution.py:253
  281.3 2.4 copy.28
  283.7 1.7 fusion
  285.4 12.8 %all_gather.15 = bf16[2,2,320,320]{3,0,2,1:T(2,128)(2,1)S(1)} all-gather(bf16[2,2,80,320]{3,0,2,1:T(2,128)(2,1)S(1)} %fusion), channel_id=1, replica_groups=mesh['frame'=32,'coil'=4] {'coil'}, dimensions={2}, use_global_device_ids=true | all-gather | bytes 1024000 | tf_op jit(solution)/shard_map/all_gather | solution.py:257
  298.2 1.1 copy.30
  (1 shorter events, 0.0 us)
Async XLA Ops:
  7.2 54.6 %copy-start = (f32[2,8]{1,0:T(2,128)S(1)}, f32[2,8]{1,0:T(2,128)}, u32[]{:S(2)}) copy-start(f32[2,8]{1,0:T(2,128)} %param.20) | copy-start | bytes 196
  7.2 51.6 %all-gather.3.cloned.1.call-start = ((), (), s32[]{:S(2)}) async-start(), calls=%async_computation.2 | async-start | bytes 2703360 | tf_op jit(solution)/shard_map/all_gather | solution.py:253
  7.9 141.5 %reduce-scatter.3.cloned.1.call-start = ((), (), s32[]{:S(2)}) async-start(), calls=%async_computation.3 | async-start | bytes 2457600 | tf_op jit(solution)/shard_map/reduce_scatter | solution.py:263
  119.8 112.7 %reduce-scatter.5.cloned.1.call-start = ((), (), s32[]{:S(2)}) async-start(), calls=%async_computation.4 | async-start | bytes 2703360 | tf_op jit(solution)/shard_map/reduce_scatter | solution.py:267
  154.6 77.8 %copy-start.1 = (f32[8,2,80,10]{2,1,3,0:T(2,128)S(1)}, f32[8,2,80,10]{2,1,3,0:T(2,128)}, u32[]{:S(2)}) copy-start(f32[8,2,80,10]{2,1,3,0:T(2,128)} %param.19) | copy-start | bytes 153604
  154.7 126.7 %all-gather.5.cloned.1.call-start = ((), (), s32[]{:S(2)}) async-start(), calls=%async_computation.5 | async-start | bytes 2703360 | tf_op jit(solution)/shard_map/all_gather | solution.py:253
Sparse Core Ops, SparseCore 0:
  10.4 48.3 all-gather.2
  119.9 29.4 reduce-scatter.2
  154.8 77.6 reduce-scatter.4
  235.4 45.8 all-gather.4
where the time goes:
time: 307 us; the launch traced here: 306 us
  waiting for transfers between devices  203 us (66%)
  Pallas kernels  42.9 us (14%)
  blocking collectives  26.1 us (9%)
  between operations  13.8 us (4%)
  local copies, waits for them, and re-layouts  10.2 us (3%)
  matrix products  6.54 us (2%)
    all_gather x2, waiting for transfers between devices, build_images(): lax.all_gather(factors, 'frame', axis=3, tiled=True)  95.2 us
    reduce_scatter x1, waiting for transfers between devices, body(): lax.psum_scatter(local_grad, 'frame', scatter_dimension=3, tiled=True)  77.8 us
    pallas_call x1, Pallas kernels, partial_residual(): pl.pallas_call(normal_kernel, out_shape=jax.ShapeDtypeStruct((frames, 2,...  42.9 us
    reduce_scatter x1, waiting for transfers between devices, body(): lax.psum_scatter(partial_value, 'coil', scatter_dimension=2, tiled=True)  29.6 us
    all_gather x2, blocking collectives, build_images(): return lax.all_gather(row_images, 'coil', axis=2, tiled=True)  26.1 us
  transfers between devices with their start and end apart: 4, of which 4 were waited for; matrix products, arithmetic and copies ran while one was open for 1% of the time, Pallas kernels for 0%

commit v1 on v0

--- a/solution.py
+++ b/solution.py
@@ -246,28 +246,358 @@
     )(level, images, sensitivity, coil_data, kernel_index, *[jnp.asarray(tables[n]) for n in TABLES])
 
 
-def build_images(factors, temporal):
-    mixed = jnp.einsum(
-        "tr,rcxy->tcxy",
-        temporal,
-        lax.all_gather(factors, "frame", axis=3, tiled=True),
-        precision=lax.Precision.HIGHEST,
-    )
-    row_images = mixed.astype(jnp.bfloat16)
-    return lax.all_gather(row_images, "coil", axis=2, tiled=True)
+def plane_shape(sp):
+    rank, _, rows, cols = sp.shape
+    return rank, rows, rows // 16, cols
+
+
+def lane_masks(cols, groups):
+    lane = lax.broadcasted_iota(jnp.int32, (16, 128), 1)
+    return lane
+
+
+def moves(block, cols, group):
+    off, start = group * cols, block * cols
+    tile, at = start // 128, start % 128
+    first = min(cols, 128 - at)
+    out = [(tile, at, off, first)]
+    if first < cols:
+        out.append((tile + 1, 0, off + first, cols - first))
+    return out
+
+
+def roll(x, shift):
+    shift = shift % 128
+    return pltpu.roll(x, shift, 1) if shift else x
+
+
+def enter(peers):
+    barrier = pltpu.get_barrier_semaphore()
+    frame, coil = lax.axis_index("frame"), lax.axis_index("coil")
+    nf, nc = lax.axis_size("frame"), lax.axis_size("coil")
+
+    def greet(i, carry):
+        pl.semaphore_signal(barrier, inc=1, device_id={"frame": lax.rem(frame + i, nf)}, device_id_type=pl.DeviceIdType.MESH)
+        return carry
+
+    lax.fori_loop(1, nf, greet, 0)
+    for step in (1, nc - 1):
+        pl.semaphore_signal(barrier, inc=1, device_id={"coil": lax.rem(coil + step, nc)}, device_id_type=pl.DeviceIdType.MESH)
+    pl.semaphore_wait(barrier, nf + 1)
+
+
+def remote(src, dst, send, recv, where):
+    return pltpu.make_async_remote_copy(src_ref=src, dst_ref=dst, send_sem=send, recv_sem=recv, device_id=where, device_id_type=pl.DeviceIdType.MESH)
+
+
+def wait_bytes(ref, sem):
+    pltpu.make_async_copy(ref, ref, sem).wait()
+
+
+def mix_and_send(weights, factors, send_buf, recv_buf, send_sem, recv_sem):
+    frame, nf = lax.axis_index("frame"), lax.axis_size("frame")
+    rank = factors.shape[0]
+
+    def piece(d, t):
+        total = weights[d, t, pl.ds(0, 1)] * factors[0]
+        for r in range(1, rank):
+            total += weights[d, t, pl.ds(r, 1)] * factors[r]
+        return total.astype(BF)
+
+    def step(i, carry):
+        d = lax.rem(frame + i, nf)
+        for t in range(2):
+            send_buf[d, t] = piece(d, t)
+        remote(send_buf.at[d], recv_buf.at[frame], send_sem, recv_sem, {"frame": d}).start()
+        return carry
+
+    lax.fori_loop(1, nf, step, 0)
+    for t in range(2):
+        recv_buf[frame, t] = piece(frame, t)
+
+
+def place_rows(recv_buf, image, t, cols):
+    coil, nf = lax.axis_index("coil"), lax.axis_size("frame")
+    size = image.shape[2]
+    rows = size // lax.axis_size("coil")
+    lane = lax.broadcasted_iota(jnp.int32, (16, 128), 1)
+    blocks = rows // 16
+    for c in range(2):
+        for rb in range(blocks):
+            tiles = [jnp.zeros((16, 128), F32) for _ in range(-(-size // 128))]
+            for f in range(nf):
+                value = recv_buf[f, t].astype(F32)
+                for tile, at, off, count in moves(f, cols, c * blocks + rb):
+                    inside = (lane >= at) & (lane < at + count)
+                    tiles[tile] = jnp.where(inside, roll(value, at - off), tiles[tile])
+            at_row = pl.multiple_of(coil * rows + rb * 16, 16)
+            for n, value in enumerate(tiles):
+                width = min(128, size - 128 * n)
+                image[t, c, pl.ds(at_row, 16), pl.ds(128 * n, width)] = value.astype(BF)[:, :width]
+
+
+def spread_rows(image, t, sems):
+    send, recv, _, _ = sems
+    coil, nc = lax.axis_index("coil"), lax.axis_size("coil")
+    rows = image.shape[2] // nc
+    mine = pl.ds(pl.multiple_of(coil * rows, 16), rows)
+    for way, step in ((0, 1), (1, nc - 1)):
+        for c in (way, 1 - way):
+            part = image.at[t, c, mine]
+            remote(part, part, send.at[t, way, c], recv.at[t, way, c], {"coil": lax.rem(coil + step, nc)}).start()
+
+
+def forward_rows(image, t, sems):
+    send, recv, send2, recv2 = sems
+    coil, nc = lax.axis_index("coil"), lax.axis_size("coil")
+    rows = image.shape[2] // nc
+    for way, step in ((0, 1), (1, nc - 1)):
+        source = lax.rem(coil + nc - step, nc)
+        part = image.at[t, way, pl.ds(pl.multiple_of(source * rows, 16), rows)]
+        wait_bytes(part, recv.at[t, way, way])
+        remote(part, part, send2.at[t, way], recv2.at[t, way], {"coil": lax.rem(coil + step, nc)}).start()
+
+
+def finish_rows(image, t, sems):
+    send, recv, send2, recv2 = sems
+    coil, nc = lax.axis_index("coil"), lax.axis_size("coil")
+    rows = image.shape[2] // nc
+    part = image.at[t, 0, pl.ds(0, rows)]
+    for way in range(2):
+        wait_bytes(part, recv.at[t, way, 1 - way])
+        wait_bytes(part, recv2.at[t, way])
+        wait_bytes(part, send2.at[t, way])
+        for c in range(2):
+            wait_bytes(part, send.at[t, way, c])
+
+
+def share_images(weights, factors, send_buf, recv_buf, image, cols, a2a, rows_sems, between=None):
+    nf = lax.axis_size("frame")
+    mix_and_send(weights, factors, send_buf, recv_buf, a2a.at[0], a2a.at[1])
+    if between is not None:
+        between()
+    wait_bytes(recv_buf.at[pl.ds(0, nf - 1)], a2a.at[1])
+    for t in range(2):
+        place_rows(recv_buf, image, t, cols)
+        spread_rows(image, t, rows_sems)
+    for t in range(2):
+        forward_rows(image, t, rows_sems)
+    for t in range(2):
+        finish_rows(image, t, rows_sems)
+    wait_bytes(recv_buf.at[pl.ds(0, nf - 1)], a2a.at[0])
+
+
+def pack_factors(spatial, factors):
+    rank, _, rows, _ = spatial.shape
+    cols = 10
+    lane = lax.broadcasted_iota(jnp.int32, (16, 128), 1)
+    blocks = rows // 16
+
+    def one(r, carry):
+        total = jnp.zeros((16, 128), F32)
+        for c in range(2):
+            for rb in range(blocks):
+                off = (c * blocks + rb) * cols
+                inside = (lane >= off) & (lane < off + cols)
+                total = jnp.where(inside, roll(spatial[r, c, pl.ds(16 * rb, 16)], off), total)
+        factors[r] = total
+        return carry
+
+    lax.fori_loop(0, rank, one, 0)
+
+
+def first_kernel(weight, spatial, image, weights, factors, send_buf, recv_buf, wsem, a2a, rs0, rs1, rs2, rs3):
+    frame, nf = lax.axis_index("frame"), lax.axis_size("frame")
+    enter(None)
+
+    def step(i, carry):
+        remote(weight, weights.at[frame], wsem.at[0], wsem.at[1], {"frame": lax.rem(frame + i, nf)}).start()
+        return carry
+
+    lax.fori_loop(1, nf, step, 0)
+    weights[frame] = weight[...]
+    pack_factors(spatial, factors)
+    wait_bytes(weights.at[pl.ds(0, nf - 1)], wsem.at[1])
+    share_images(weights, factors, send_buf, recv_buf, image, 10, a2a, (rs0, rs1, rs2, rs3))
+    wait_bytes(weights.at[pl.ds(0, nf - 1)], wsem.at[0])
+
+
+def row_sems():
+    return [
+        pltpu.SemaphoreType.DMA((2, 2, 2)),
+        pltpu.SemaphoreType.DMA((2, 2, 2)),
+        pltpu.SemaphoreType.DMA((2, 2)),
+        pltpu.SemaphoreType.DMA((2, 2)),
+    ]
+
+
+def first_images(spatial, weight, size):
+    nf = lax.axis_size("frame")
+    rank = spatial.shape[0]
+    vm = pl.BlockSpec(memory_space=pltpu.VMEM)
+    return pl.pallas_call(
+        first_kernel,
+        out_shape=(jax.ShapeDtypeStruct((2, 2, size, size), BF), jax.ShapeDtypeStruct((nf, 2, rank, 128), F32)),
+        in_specs=[vm, vm],
+        out_specs=(vm, vm),
+        scratch_shapes=[
+            pltpu.VMEM((rank, 16, 128), F32),
+            pltpu.VMEM((nf, 2, 16, 128), BF),
+            pltpu.VMEM((nf, 2, 16, 128), BF),
+            pltpu.SemaphoreType.DMA((2,)),
+            pltpu.SemaphoreType.DMA((2,)),
+        ] + row_sems(),
+        compiler_params=pltpu.CompilerParams(vmem_limit_bytes=40 * 2**20, collective_id=0, has_side_effects=True),
+    )(weight, spatial)
+
+
+def reduce_start(part, t, xa, xd, sems):
+    s1, r1, s2, r2, s3, r3 = sems
+    coil, nc = lax.axis_index("coil"), lax.axis_size("coil")
+    rows = part.shape[2] // nc
+    far = pl.ds(pl.multiple_of(lax.rem(coil + 2, nc) * rows, 16), rows)
+    for way, step in ((0, 1), (1, nc - 1)):
+        to = lax.rem(coil + step, nc)
+        near = pl.ds(pl.multiple_of(to * rows, 16), rows)
+        remote(part.at[t, way, far], xa.at[t, way], s1.at[t, way], r1.at[t, way], {"coil": to}).start()
+        remote(part.at[t, 1 - way, near], xd.at[t, way], s2.at[t, way], r2.at[t, way], {"coil": to}).start()
+
+
+def reduce_forward(part, t, xa, xsum, xs, sems):
+    s1, r1, s2, r2, s3, r3 = sems
+    coil, nc = lax.axis_index("coil"), lax.axis_size("coil")
+    rows = part.shape[2] // nc
+    for way, step in ((0, 1), (1, nc - 1)):
+        to = lax.rem(coil + step, nc)
+        near = pl.ds(pl.multiple_of(to * rows, 16), rows)
+        wait_bytes(xa.at[t, way], r1.at[t, way])
+        xsum[t, way] = xa[t, way] + part[t, way, near]
+        remote(xsum.at[t, way], xs.at[t, way], s3.at[t, way], r3.at[t, way], {"coil": to}).start()
+
+
+def reduce_finish(part, t, xd, xs, total, sems):
+    s1, r1, s2, r2, s3, r3 = sems
+    coil, nc = lax.axis_index("coil"), lax.axis_size("coil")
+    size = part.shape[3]
+    rows = part.shape[2] // nc
+    mine = pl.ds(pl.multiple_of(coil * rows, 16), rows)
+    for way in range(2):
+        wait_bytes(xs.at[t, way], r3.at[t, way])
+        wait_bytes(xd.at[t, 1 - way], r2.at[t, 1 - way])
+        total[t, way, :, pl.ds(0, size)] = part[t, way, mine] + xs[t, way] + xd[t, 1 - way]
+
+
+def send_columns(total, t, send_buf, recv_buf, sems, cols):
+    frame, nf = lax.axis_index("frame"), lax.axis_size("frame")
+    rows = total.shape[2]
+    blocks = rows // 16
+    lane = lax.broadcasted_iota(jnp.int32, (16, 128), 1)
+    for f in range(nf):
+        value = jnp.zeros((16, 128), F32)
+        for c in range(2):
+            for rb in range(blocks):
+                for tile, at, off, count in moves(f, cols, c * blocks + rb):
+                    inside = (lane >= off) & (lane < off + count)
+                    value = jnp.where(inside, roll(total[t, c, pl.ds(16 * rb, 16), pl.ds(128 * tile, 128)], off - at), value)
+        send_buf[t, f] = value
+
+    def step(i, carry):
+        d = lax.rem(frame + i, nf)
+        remote(send_buf.at[t, d], recv_buf.at[t, frame], sems.at[0, t], sems.at[1, t], {"frame": d}).start()
+        return carry
+
+    lax.fori_loop(1, nf, step, 0)
+    recv_buf[t, frame] = send_buf[t, frame]
+
+
+def gradient_step(weights, recv_buf, t, grad):
+    nf = lax.axis_size("frame")
+    rank = grad.shape[0]
+
+    def step(f, acc):
+        value = recv_buf[t, f]
+        return tuple(acc[r] + weights[f, t, pl.ds(r, 1)] * value for r in range(rank))
+
+    acc = lax.fori_loop(0, nf, step, tuple(jnp.zeros((16, 128), F32) for _ in range(rank)))
+    for r in range(rank):
+        grad[r] = acc[r] if t == 0 else grad[r] + acc[r]
+
+
+def unpack_factors(factors, spatial):
+    rank, _, rows, cols = spatial.shape
+    blocks = rows // 16
+
+    def one(r, carry):
+        value = factors[r]
+        for c in range(2):
+            for rb in range(blocks):
+                spatial[r, c, pl.ds(16 * rb, 16)] = roll(value, -(c * blocks + rb) * cols)[:, :cols]
+        return carry
+
+    lax.fori_loop(0, rank, one, 0)
+
+
+def last_kernel(part, weights, spatial, spatial_next, image, factors, grad, xa, xd, xsum, xs, total, rsend, rrecv, send_buf, recv_buf, a2a, rsem, s1, r1, s2, r2, s3, r3, rs0, rs1, rs2, rs3):
+    frame, nf = lax.axis_index("frame"), lax.axis_size("frame")
+    cols = spatial_next.shape[3]
+    sems = (s1, r1, s2, r2, s3, r3)
+    enter(None)
+    for t in range(2):
+        reduce_start(part, t, xa, xd, sems)
+    pack_factors(spatial, factors)
+    for t in range(2):
+        reduce_forward(part, t, xa, xsum, xs, sems)
+    for t in range(2):
+        reduce_finish(part, t, xd, xs, total, sems)
+        send_columns(total, t, rsend, rrecv, rsem, cols)
+    for t in range(2):
+        wait_bytes(rrecv.at[t, pl.ds(0, nf - 1)], rsem.at[1, t])
+        gradient_step(weights, rrecv, t, grad)
+    for r in range(factors.shape[0]):
+        factors[r] = factors[r] - STEP_SIZE * grad[r]
+    share_images(weights, factors, send_buf, recv_buf, image, cols, a2a, (rs0, rs1, rs2, rs3), lambda: unpack_factors(factors, spatial_next))
+    for t in range(2):
+        wait_bytes(rrecv.at[t, pl.ds(0, nf - 1)], rsem.at[0, t])
+        for way in range(2):
+            for sem in (s1, s2, s3):
+                wait_bytes(xa.at[t, way], sem.at[t, way])
+
+
+def update(part, weights, padded, spatial):
+    nf = lax.axis_size("frame")
+    size = part.shape[2]
+    rank, _, rows, cols = spatial.shape
+    vm = pl.BlockSpec(memory_space=pltpu.VMEM)
+    block = pltpu.VMEM((2, 2, rows, size), F32)
+    return pl.pallas_call(
+        last_kernel,
+        out_shape=(jax.ShapeDtypeStruct(spatial.shape, F32), jax.ShapeDtypeStruct((2, 2, size, size), BF)),
+        in_specs=[vm, vm, vm],
+        out_specs=(vm, vm),
+        scratch_shapes=[
+            pltpu.VMEM((rank, 16, 128), F32),
+            pltpu.VMEM((rank, 16, 128), F32),
+            block, block, block, block,
+            pltpu.VMEM((2, 2, rows, -(-size // 128) * 128), F32),
+            pltpu.VMEM((2, nf, 16, 128), F32),
+            pltpu.VMEM((2, nf, 16, 128), F32),
+            pltpu.VMEM((nf, 2, 16, 128), BF),
+            pltpu.VMEM((nf, 2, 16, 128), BF),
+            pltpu.SemaphoreType.DMA((2,)),
+            pltpu.SemaphoreType.DMA((2, 2)),
+        ] + [pltpu.SemaphoreType.DMA((2, 2))] * 6 + row_sems(),
+        compiler_params=pltpu.CompilerParams(vmem_limit_bytes=40 * 2**20, collective_id=1, has_side_effects=True),
+    )(part, weights, padded)
 
 
 def body(spatial, temporal, sensitivity, coil_data, kernel_index, kernel_level):
-    full_images = build_images(spatial, temporal)
+    size = sensitivity.shape[2]
+    cols = spatial.shape[3]
+    padded = jnp.pad(spatial, ((0, 0), (0, 0), (0, 0), (0, 128 - cols)))
+    weight = jnp.broadcast_to(temporal[:, :, None], temporal.shape + (128,))
+    full_images, weights = first_images(padded, weight, size)
     partial_value = partial_residual(full_images, sensitivity, coil_data, kernel_index, kernel_level)
-    rows_residual = lax.psum_scatter(partial_value, "coil", scatter_dimension=2, tiled=True)
-    local_grad = jnp.einsum(
-        "tr,tcxy->rcxy", temporal, rows_residual, precision=lax.Precision.HIGHEST
-    )
-    gradient = lax.psum_scatter(local_grad, "frame", scatter_dimension=3, tiled=True)
-    spatial_next = spatial - STEP_SIZE * gradient
-    images = build_images(spatial_next, temporal)
-    return (spatial_next, images)
+    return update(partial_value, weights, padded, spatial)
 
 
 def solution(mesh):

time: 307 us -> 129 us (0.42)
  waiting for transfers between devices: 203 us -> 0 us
  Pallas kernels: 42.9 us -> 121 us
  blocking collectives: 26.1 us -> 0 us
  between operations: 13.8 us -> 0.67 us
  matrix products: 6.54 us -> 0 us
  local copies, waits for them, and re-layouts: 10.2 us -> 6.25 us
    reduce_scatter x2 -> x0, waiting for transfers between devices: 107 us -> none  [the longest x1 77.8 us: body(): lax.psum_scatter(local_grad, 'frame', scatter_dimension=3, tiled=True)]
    all_gather x2 -> x0, waiting for transfers between devices: 95.2 us -> none  [build_images(): lax.all_gather(factors, 'frame', axis=3, tiled=True)]
    pallas_call x0 -> x2, Pallas kernels: none -> 78.9 us  [the longest x1 46.3 us: update(): pl.pallas_call(last_kernel, out_shape=(jax.ShapeDtypeStruct(spatial.shape...]
    all_gather x2 -> x0, blocking collectives: 26.1 us -> none  [build_images(): return lax.all_gather(row_images, 'coil', axis=2, tiled=True)]
    dot_general x3 -> x0, matrix products: 6.54 us -> none  [the longest x2 3.49 us: build_images(): jnp.einsum('tr,rcxy->tcxy', temporal, lax.all_gather(factors, 'frame', ax...]
    all_gather x2 -> x0, local copies, waits for them, and re-layouts: 5.38 us -> none  [build_images(): lax.all_gather(factors, 'frame', axis=3, tiled=True)]
  transfers between devices with their start and end apart: 4 -> 0, of which waited for: 4 -> 0; matrix products, arithmetic and copies ran while one was open for 1% -> 0% of each run, Pallas kernels for 0% -> 0%
where the time goes in v1:
time: 129 us
  Pallas kernels  121 us (94%)
  local copies, waits for them, and re-layouts  6.25 us (5%)
    pallas_call x1, Pallas kernels, update(): pl.pallas_call(last_kernel, out_shape=(jax.ShapeDtypeStruct(spatial.shape...  46.3 us
    pallas_call x1, Pallas kernels, partial_residual(): pl.pallas_call(normal_kernel, out_shape=jax.ShapeDtypeStruct((frames, 2,...  41.9 us
    pallas_call x1, Pallas kernels, first_images(): pl.pallas_call(first_kernel, out_shape=(jax.ShapeDtypeStruct((2, 2, size,...  32.6 us
    unnamed x6, local copies, waits for them, and re-layouts  4.58 us

profile of v1, /device:TPU:1, one launch (start us, length us, event | category | flops | bytes accessed | tf_op | source)
XLA Modules:
  0.0 129.0 jit_solution(15254882270906494682)
XLA Ops:
  0.6 1.2 broadcast_multiply_fusion.level
  1.9 0.7 broadcast_in_dim.2.weight
  2.6 1.1 copy.21
  3.8 32.6 %shard_map.194 = (bf16[2,2,320,320]{3,2,1,0:T(8,128)(2,1)S(1)}, f32[32,2,8,128]{3,2,1,0:T(8,128)S(1)}) custom-call(f32[2,8,128]{2,1,0:T(8,128)S(1)} %broadcast_in_dim.2.weight, f32[8,2,80,128]{3,2,1,0:T(8,128)S(1)} %pad.4.spatial), custom_call_target="tpu_custom_call" | custom-call | tf_op jit(solution)/shard_map/pallas_call | solution.py:438
  36.4 0.0 copy-start.1
  36.4 0.9 copy-done.1
  37.3 41.9 %shard_map.195.part = f32[2,2,320,320]{3,2,1,0:T(8,128)} custom-call(f32[2,8]{1,0:T(2,128)} %broadcast_multiply_fusion.level, bf16[2,2,320,320]{3,2,1,0:T(8,128)(2,1)} %copy-done.1, bf16[2,2,320,320]{3,2,1,0:T(8,128)(2,1)} %sens.1, bf16[2,2,2,320,320]{4,3,2,1,0:T(8,128)(2,1)} %data.1, s32[2,640,640]{2,1,0:T(8,128)} %index.1, ...), custom_call_target="tpu_custom_call" | custom-call | tf_op jit(solution)/shard_map/pallas_call | solution.py:222
  79.3 0.0 copy-start
  79.3 1.5 %copy-done = f32[2,2,320,320]{3,2,1,0:T(8,128)S(1)} copy-done((f32[2,2,320,320]{3,2,1,0:T(8,128)S(1)}, f32[2,2,320,320]{3,2,1,0:T(8,128)}, u32[]{:S(2)}) %copy-start) | copy-done | bytes 1638424
  80.8 46.3 %shard_map.196 = (f32[8,2,80,10]{3,2,1,0:T(8,128)S(1)}, bf16[2,2,320,320]{3,2,1,0:T(8,128)(2,1)S(1)}) custom-call(f32[2,2,320,320]{3,2,1,0:T(8,128)S(1)} %copy-done, f32[32,2,8,128]{3,2,1,0:T(8,128)S(1)} %get-tuple-element.5.weights, f32[8,2,80,128]{3,2,1,0:T(8,128)S(1)} %pad.4.spatial), custom_call_target="tpu_custom_call" | custom-call | tf_op jit(solution)/shard_map/pallas_call | solution.py:572
  127.1 0.9 copy.22
  128.0 0.9 copy.24
  (1 shorter events, 0.0 us)
Async XLA Ops:
  36.4 0.9 copy-start.1
  79.3 1.5 %copy-start = (f32[2,2,320,320]{3,2,1,0:T(8,128)S(1)}, f32[2,2,320,320]{3,2,1,0:T(8,128)}, u32[]{:S(2)}) copy-start(f32[2,2,320,320]{3,2,1,0:T(8,128)} %shard_map.195.part) | copy-start | bytes 4915204

commit v2 on v1

v2 whole, which is shorter than its diff:
```python
import types

import jax
import jax.numpy as jnp
import ml_dtypes
import numpy as np
from jax import lax
from jax.experimental import pallas as pl
from jax.experimental.pallas import tpu as pltpu
from jax.sharding import PartitionSpec as P

STEP_SIZE = 0.15
BF = jnp.bfloat16
F32 = jnp.float32


def halves(table):
    high = table.astype(ml_dtypes.bfloat16)
    low = (table - high.astype(np.float64)).astype(ml_dtypes.bfloat16)
    return high, low


def make_tables(size):
    half = size // 2
    slots = -(-(size + 1) // 128) * 128
    rows = -(-(size + 1) // 16) * 16
    p = np.arange(half) + 0.5
    k = np.arange(slots)
    valid = (k <= size).astype(np.float64)
    angle = np.pi / size * np.outer(p, k)
    cos, sin = np.cos(angle) * valid, np.sin(angle) * valid
    cos[:, size] = 0.0
    sin[:, 0] = 0.0
    weight = np.where((k == 0) | (k == size), 0.5, 1.0)
    out = {}
    for name, tab in (("c", cos), ("s", sin)):
        hi, lo = halves(tab)
        out["f1" + name] = np.concatenate([hi, lo], axis=1)
        rhi, rlo = hi[:, :rows].T, lo[:, :rows].T
        out["f2" + name] = np.concatenate([rhi, rhi, rlo], axis=1)
        whi, wlo = halves(tab * weight)
        out["i1" + name] = np.concatenate([whi[:, :rows], whi[:, :rows], wlo[:, :rows]], axis=1)
        parts = []
        for j in range(0, slots, 128):
            parts += [whi.T[j:j + 128], whi.T[j:j + 128], wlo.T[j:j + 128]]
        out["i2" + name] = np.concatenate(parts, axis=0)
    wide = -(-half // 128) * 128
    place = np.zeros((size, 2 * wide))
    q = np.arange(half)
    place[half + q, q] = 1
    place[half - 1 - q, wide + q] = 1
    out["place"] = place.astype(ml_dtypes.bfloat16)
    out["unplace"] = place.T.astype(ml_dtypes.bfloat16)
    out["flip"] = np.eye(half)[::-1].astype(ml_dtypes.bfloat16)
    mirror = np.zeros((2 * size, slots))
    kk = np.arange(size + 1)
    mirror[(2 * size - kk) % (2 * size), kk] = 1
    out["mirror"] = mirror.astype(ml_dtypes.bfloat16)
    out["mirror_rows"] = mirror.T[:rows].astype(ml_dtypes.bfloat16)
    return out


TABLES = ("f1c", "f1s", "f2c", "f2s", "i1c", "i1s", "i2c", "i2s", "place", "unplace", "flip", "mirror", "mirror_rows")


def mm(a, b):
    return jnp.dot(a, b, preferred_element_type=F32)


def split(x):
    high = x.astype(BF)
    low = (x - high.astype(F32)).astype(BF)
    return high, low


def kernel_quads(s, level, t):
    rows = s.f2c.shape[0]
    slots = s.mirror.shape[1]
    ib = s.index[t].astype(F32).astype(BF)
    flipped = mm(ib, s.mirror[...]).astype(BF)
    low = mm(s.mirror_rows[...], jnp.concatenate([ib[:, :slots], flipped], axis=1))
    quads = (ib[:rows, :slots].astype(F32), flipped[:rows].astype(F32), low[:, :slots], low[:, slots:])
    for n, quad in enumerate(quads):
        value = jnp.full(quad.shape, level[t, 0], F32)
        for m in range(1, level.shape[1]):
            value = jnp.where(quad > m - 0.5, level[t, m], value)
        s.kq[t, n] = value


def folded(s, x):
    half = s.flip.shape[0]
    left = mm(s.flip[...], x[:half]).astype(BF)
    return mm(jnp.concatenate([x[half:], left], axis=0), s.place[...])


def fold_data(s, t):
    for c in range(s.sens.shape[0]):
        dr, di = folded(s, s.data[t, c, 0]), folded(s, s.data[t, c, 1])
        sr, si = s.sf[c, 0], s.sf[c, 1]
        gr, gi = -(sr * dr + si * di), si * dr - sr * di
        if c:
            gr, gi = s.res[t, 0] + gr, s.res[t, 1] + gi
        s.res[t, 0] = gr
        s.res[t, 1] = gi


def unfold(s, t):
    half = s.flip.shape[0]
    for h in range(2):
        high, low = split(s.res[t, h])
        cols = mm(high, s.unplace[...]) + mm(low, s.unplace[...])
        s.part[t, h, pl.ds(half, half)] = cols[:half]
        high, low = split(cols[half:])
        s.part[t, h, pl.ds(0, half)] = mm(s.flip[...], high) + mm(s.flip[...], low)


def run_pair(s, t, c):
    half = s.flip.shape[0]
    wide = s.place.shape[1] // 2
    rows = s.f2c.shape[0]
    slots = s.mirror.shape[1]
    chunks = slots // 128
    for r in range(0, half, 16):
        parts = {}
        for a, row in (("R", r), ("L", half + r)):
            for b, col in (("R", 0), ("L", wide)):
                sl = (pl.ds(row, 16), pl.ds(col, half))
                sr, si = s.sf[c, 0, sl[0], sl[1]], s.sf[c, 1, sl[0], sl[1]]
                ir, ii = s.imf[t, 0, sl[0], sl[1]], s.imf[t, 1, sl[0], sl[1]]
                parts[a + b] = (sr * ir - si * ii, sr * ii + si * ir)
        for h in range(2):
            rr, rl, lr, ll = (parts[n][h] for n in ("RR", "RL", "LR", "LL"))
            re, ro, le, lo = rr + rl, rr - rl, lr + ll, lr - ll
            for k, (xc, xs) in enumerate(((re + le, ro + lo), (re - le, ro - lo))):
                at = (2 * k + h) * half + r
                hc, wc = split(xc)
                hs, ws = split(xs)
                s.lc[0, pl.ds(at, 16)] = hc
                s.lc[1, pl.ds(at, 16)] = wc
                s.ls[0, pl.ds(at, 16)] = hs
                s.ls[1, pl.ds(at, 16)] = ws
    for n, (lref, tab) in enumerate(((s.lc, s.f1c), (s.ls, s.f1s))):
        first = mm(lref[0], tab[:, :slots]) + mm(lref[0], tab[:, slots:]) + mm(lref[1], tab[:, :slots])
        for k, dest in enumerate((s.ge, s.go)):
            for h in range(2):
                part = first[(2 * k + h) * half:(2 * k + h + 1) * half]
                high, low = split(part)
                for j in range(chunks):
                    lanes = pl.ds((2 * n + h) * 128, 128)
                    dest[j, pl.ds(0, half), lanes] = high[:, j * 128:(j + 1) * 128]
                    dest[j, pl.ds(half, half), lanes] = low[:, j * 128:(j + 1) * 128]
                    dest[j, pl.ds(2 * half, half), lanes] = high[:, j * 128:(j + 1) * 128]
    for j in range(chunks):
        s.spa[j] = mm(s.f2c[...], s.ge[j])
        s.spb[j] = mm(s.f2s[...], s.go[j])
        for r in range(0, rows, 16):
            rs = pl.ds(r, 16)
            aar, aai, abr, abi = (s.spa[j, rs, pl.ds(128 * m, 128)] for m in range(4))
            bar, bai, bbr, bbi = (s.spb[j, rs, pl.ds(128 * m, 128)] for m in range(4))
            kpp, kpm, kmp, kmm = (s.kq[t, m, rs, pl.ds(128 * j, 128)] for m in range(4))
            ur, ui, vr, vi = aar - bbr, aai - bbi, aar + bbr, aai + bbi
            wr, wi, qr, qi = abr + bar, abi + bai, abr - bar, abi - bai
            ppr, ppi = kpp * (ur + wi), kpp * (ui - wr)
            mmr, mmi = kmm * (ur - wi), kmm * (ui + wr)
            pmr, pmi = kpm * (vr - qi), kpm * (vi + qr)
            mpr, mpi = kmp * (vr + qi), kmp * (vi - qr)
            s1r, s1i, s2r, s2i = ppr + mmr, ppi + mmi, pmr + mpr, pmi + mpi
            d1r, d1i, d2r, d2i = ppr - mmr, ppi - mmi, pmr - mpr, pmi - mpi
            for dest, vals in ((s.za, (s1r + s2r, s1i + s2i, d2i - d1i, d1r - d2r)), (s.zb, (-(d1i + d2i), d1r + d2r, s2r - s1r, s2i - s1i))):
                for m, value in enumerate(vals):
                    high, low = split(value)
                    lanes = pl.ds(128 * m, 128)
                    dest[j, pl.ds(r, 16), lanes] = high
                    dest[j, pl.ds(rows + r, 16), lanes] = low
                    dest[j, pl.ds(2 * rows + r, 16), lanes] = high
        for n, (tab, src) in enumerate(((s.i1c, s.za), (s.i1s, s.zb))):
            high, low = split(mm(tab[...], src[j]))
            for m in range(4):
                dest = s.lhc if m < 2 else s.lhs
                rs = pl.ds((2 * n + m % 2) * half, half)
                for place_at, value in enumerate((high, low, high)):
                    dest[rs, pl.ds(j * 384 + place_at * 128, 128)] = value[:, 128 * m:128 * (m + 1)]
    s.oc[...] = mm(s.lhc[...], s.i2c[...])
    s.osn[...] = mm(s.lhs[...], s.i2s[...])
    for r in range(0, half, 16):
        quad = {}
        for h in range(2):
            ee, oe = s.oc[pl.ds(h * half + r, 16)], s.oc[pl.ds((2 + h) * half + r, 16)]
            eo, oo = s.osn[pl.ds(h * half + r, 16)], s.osn[pl.ds((2 + h) * half + r, 16)]
            quad["RR", h] = (ee + oe) + (eo + oo)
            quad["RL", h] = (ee + oe) - (eo + oo)
            quad["LR", h] = (ee - oe) + (eo - oo)
            quad["LL", h] = (ee - oe) - (eo - oo)
        for a, row in (("R", r), ("L", half + r)):
            for b, col in (("R", 0), ("L", wide)):
                sl = (pl.ds(row, 16), pl.ds(col, half))
                sr, si = s.sf[c, 0, sl[0], sl[1]], s.sf[c, 1, sl[0], sl[1]]
                yr, yi = quad[a + b, 0], quad[a + b, 1]
                s.res[t, 0, sl[0], sl[1]] += sr * yr + si * yi
                s.res[t, 1, sl[0], sl[1]] += sr * yi - si * yr


def plane_shape(sp):
    rank, _, rows, cols = sp.shape
    return rank, rows, rows // 16, cols


def lane_masks(cols, groups):
    lane = lax.broadcasted_iota(jnp.int32, (16, 128), 1)
    return lane


def moves(block, cols, group):
    off, start = group * cols, block * cols
    tile, at = start // 128, start % 128
    first = min(cols, 128 - at)
    out = [(tile, at, off, first)]
    if first < cols:
        out.append((tile + 1, 0, off + first, cols - first))
    return out


def roll(x, shift):
    shift = shift % 128
    return pltpu.roll(x, shift, 1) if shift else x


def enter(peers):
    barrier = pltpu.get_barrier_semaphore()
    frame, coil = lax.axis_index("frame"), lax.axis_index("coil")
    nf, nc = lax.axis_size("frame"), lax.axis_size("coil")

    def greet(i, carry):
        pl.semaphore_signal(barrier, inc=1, device_id={"frame": lax.rem(frame + i, nf)}, device_id_type=pl.DeviceIdType.MESH)
        return carry

    lax.fori_loop(1, nf, greet, 0)
    for step in (1, nc - 1):
        pl.semaphore_signal(barrier, inc=1, device_id={"coil": lax.rem(coil + step, nc)}, device_id_type=pl.DeviceIdType.MESH)
    pl.semaphore_wait(barrier, nf + 1)


def remote(src, dst, send, recv, where):
    return pltpu.make_async_remote_copy(src_ref=src, dst_ref=dst, send_sem=send, recv_sem=recv, device_id=where, device_id_type=pl.DeviceIdType.MESH)


def wait_bytes(ref, sem):
    pltpu.make_async_copy(ref, ref, sem).wait()


def mix_and_send(weights, factors, send_buf, recv_buf, send_sem, recv_sem):
    frame, nf = lax.axis_index("frame"), lax.axis_size("frame")
    rank = factors.shape[0]

    def piece(d, t):
        total = weights[d, t, pl.ds(0, 1)] * factors[0]
        for r in range(1, rank):
            total += weights[d, t, pl.ds(r, 1)] * factors[r]
        return total.astype(BF)

    def step(i, carry):
        d = lax.rem(frame + i, nf)
        for t in range(2):
            send_buf[d, t] = piece(d, t)
        remote(send_buf.at[d], recv_buf.at[frame], send_sem, recv_sem, {"frame": d}).start()
        return carry

    lax.fori_loop(1, nf, step, 0)
    for t in range(2):
        recv_buf[frame, t] = piece(frame, t)


def place_rows(recv_buf, image, t, cols):
    coil, nf = lax.axis_index("coil"), lax.axis_size("frame")
    size = image.shape[2]
    rows = size // lax.axis_size("coil")
    lane = lax.broadcasted_iota(jnp.int32, (16, 128), 1)
    blocks = rows // 16
    for c in range(2):
        for rb in range(blocks):
            tiles = [jnp.zeros((16, 128), F32) for _ in range(-(-size // 128))]
            for f in range(nf):
                value = recv_buf[f, t].astype(F32)
                for tile, at, off, count in moves(f, cols, c * blocks + rb):
                    inside = (lane >= at) & (lane < at + count)
                    tiles[tile] = jnp.where(inside, roll(value, at - off), tiles[tile])
            at_row = pl.multiple_of(coil * rows + rb * 16, 16)
            for n, value in enumerate(tiles):
                width = min(128, size - 128 * n)
                image[t, c, pl.ds(at_row, 16), pl.ds(128 * n, width)] = value.astype(BF)[:, :width]


def spread_rows(image, t, sems):
    send, recv, _, _ = sems
    coil, nc = lax.axis_index("coil"), lax.axis_size("coil")
    rows = image.shape[2] // nc
    mine = pl.ds(pl.multiple_of(coil * rows, 16), rows)
    for way, step in ((0, 1), (1, nc - 1)):
        for c in (way, 1 - way):
            part = image.at[t, c, mine]
            remote(part, part, send.at[t, way, c], recv.at[t, way, c], {"coil": lax.rem(coil + step, nc)}).start()


def forward_rows(image, t, sems):
    send, recv, send2, recv2 = sems
    coil, nc = lax.axis_index("coil"), lax.axis_size("coil")
    rows = image.shape[2] // nc
    for way, step in ((0, 1), (1, nc - 1)):
        source = lax.rem(coil + nc - step, nc)
        part = image.at[t, way, pl.ds(pl.multiple_of(source * rows, 16), rows)]
        wait_bytes(part, recv.at[t, way, way])
        remote(part, part, send2.at[t, way], recv2.at[t, way], {"coil": lax.rem(coil + step, nc)}).start()


def finish_rows(image, t, sems):
    send, recv, send2, recv2 = sems
    coil, nc = lax.axis_index("coil"), lax.axis_size("coil")
    rows = image.shape[2] // nc
    part = image.at[t, 0, pl.ds(0, rows)]
    for way in range(2):
        wait_bytes(part, recv.at[t, way, 1 - way])
        wait_bytes(part, recv2.at[t, way])
        wait_bytes(part, send2.at[t, way])
        for c in range(2):
            wait_bytes(part, send.at[t, way, c])


def share_images(weights, factors, send_buf, recv_buf, image, cols, a2a, rows_sems, between=None):
    nf = lax.axis_size("frame")
    mix_and_send(weights, factors, send_buf, recv_buf, a2a.at[0], a2a.at[1])
    if between is not None:
        between()
    wait_bytes(recv_buf.at[pl.ds(0, nf - 1)], a2a.at[1])
    for t in range(2):
        place_rows(recv_buf, image, t, cols)
        spread_rows(image, t, rows_sems)
    for t in range(2):
        forward_rows(image, t, rows_sems)
    for t in range(2):
        finish_rows(image, t, rows_sems)
    wait_bytes(recv_buf.at[pl.ds(0, nf - 1)], a2a.at[0])


def pack_factors(spatial, factors):
    rank, _, rows, _ = spatial.shape
    cols = 10
    lane = lax.broadcasted_iota(jnp.int32, (16, 128), 1)
    blocks = rows // 16

    def one(r, carry):
        total = jnp.zeros((16, 128), F32)
        for c in range(2):
            for rb in range(blocks):
                off = (c * blocks + rb) * cols
                inside = (lane >= off) & (lane < off + cols)
                total = jnp.where(inside, roll(spatial[r, c, pl.ds(16 * rb, 16)], off), total)
        factors[r] = total
        return carry

    lax.fori_loop(0, rank, one, 0)


def row_sems():
    return [
        pltpu.SemaphoreType.DMA((2, 2, 2)),
        pltpu.SemaphoreType.DMA((2, 2, 2)),
        pltpu.SemaphoreType.DMA((2, 2)),
        pltpu.SemaphoreType.DMA((2, 2)),
    ]


def reduce_start(part, t, xa, xd, sems):
    s1, r1, s2, r2, s3, r3 = sems
    coil, nc = lax.axis_index("coil"), lax.axis_size("coil")
    rows = part.shape[2] // nc
    far = pl.ds(pl.multiple_of(lax.rem(coil + 2, nc) * rows, 16), rows)
    for way, step in ((0, 1), (1, nc - 1)):
        to = lax.rem(coil + step, nc)
        near = pl.ds(pl.multiple_of(to * rows, 16), rows)
        remote(part.at[t, way, far], xa.at[t, way], s1.at[t, way], r1.at[t, way], {"coil": to}).start()
        remote(part.at[t, 1 - way, near], xd.at[t, way], s2.at[t, way], r2.at[t, way], {"coil": to}).start()


def reduce_forward(part, t, xa, xsum, xs, sems):
    s1, r1, s2, r2, s3, r3 = sems
    coil, nc = lax.axis_index("coil"), lax.axis_size("coil")
    rows = part.shape[2] // nc
    for way, step in ((0, 1), (1, nc - 1)):
        to = lax.rem(coil + step, nc)
        near = pl.ds(pl.multiple_of(to * rows, 16), rows)
        wait_bytes(xa.at[t, way], r1.at[t, way])
        xsum[t, way] = xa[t, way] + part[t, way, near]
        remote(xsum.at[t, way], xs.at[t, way], s3.at[t, way], r3.at[t, way], {"coil": to}).start()


def reduce_finish(part, t, xd, xs, total, sems):
    s1, r1, s2, r2, s3, r3 = sems
    coil, nc = lax.axis_index("coil"), lax.axis_size("coil")
    size = part.shape[3]
    rows = part.shape[2] // nc
    mine = pl.ds(pl.multiple_of(coil * rows, 16), rows)
    for way in range(2):
        wait_bytes(xs.at[t, way], r3.at[t, way])
        wait_bytes(xd.at[t, 1 - way], r2.at[t, 1 - way])
        total[t, way, :, pl.ds(0, size)] = part[t, way, mine] + xs[t, way] + xd[t, 1 - way]


def send_columns(total, t, send_buf, recv_buf, sems, cols):
    frame, nf = lax.axis_index("frame"), lax.axis_size("frame")
    rows = total.shape[2]
    blocks = rows // 16
    lane = lax.broadcasted_iota(jnp.int32, (16, 128), 1)
    for f in range(nf):
        value = jnp.zeros((16, 128), F32)
        for c in range(2):
            for rb in range(blocks):
                for tile, at, off, count in moves(f, cols, c * blocks + rb):
                    inside = (lane >= off) & (lane < off + count)
                    value = jnp.where(inside, roll(total[t, c, pl.ds(16 * rb, 16), pl.ds(128 * tile, 128)], off - at), value)
        send_buf[t, f] = value

    def step(i, carry):
        d = lax.rem(frame + i, nf)
        remote(send_buf.at[t, d], recv_buf.at[t, frame], sems.at[0, t], sems.at[1, t], {"frame": d}).start()
        return carry

    lax.fori_loop(1, nf, step, 0)
    recv_buf[t, frame] = send_buf[t, frame]


def gradient_step(weights, recv_buf, t, grad):
    nf = lax.axis_size("frame")
    rank = grad.shape[0]

    def step(f, acc):
        value = recv_buf[t, f]
        return tuple(acc[r] + weights[f, t, pl.ds(r, 1)] * value for r in range(rank))

    acc = lax.fori_loop(0, nf, step, tuple(jnp.zeros((16, 128), F32) for _ in range(rank)))
    for r in range(rank):
        grad[r] = acc[r] if t == 0 else grad[r] + acc[r]


def unpack_factors(factors, spatial):
    rank, _, rows, cols = spatial.shape
    blocks = rows // 16

    def one(r, carry):
        value = factors[r]
        for c in range(2):
            for rb in range(blocks):
                spatial[r, c, pl.ds(16 * rb, 16)] = roll(value, -(c * blocks + rb) * cols)[:, :cols]
        return carry

    lax.fori_loop(0, rank, one, 0)


LOCAL = ("spatial", "index", "sens", "data") + TABLES


def whole_kernel(weight, level, *refs, **scratch):
    s = types.SimpleNamespace(**scratch)
    sources, (spatial_next, image) = refs[:len(LOCAL)], refs[len(LOCAL):]
    frame, nf = lax.axis_index("frame"), lax.axis_size("frame")
    cols = spatial_next.shape[3]
    copies = {}
    for n, (name, source) in enumerate(zip(LOCAL, sources)):
        copies[name] = pltpu.make_async_copy(source, scratch[name], s.lsem.at[n])
        copies[name].start()

    def ready(*names):
        for name in names:
            copies[name].wait()

    enter(None)

    def exchange(i, carry):
        remote(weight, s.weights.at[frame], s.wsem.at[0], s.wsem.at[1], {"frame": lax.rem(frame + i, nf)}).start()
        return carry

    lax.fori_loop(1, nf, exchange, 0)
    s.weights[frame] = weight[...]
    ready("spatial")
    pack_factors(s.spatial, s.factors)
    ready("index", *TABLES)
    kernel_quads(s, level, 0)
    wait_bytes(s.weights.at[pl.ds(0, nf - 1)], s.wsem.at[1])
    mix_and_send(s.weights, s.factors, s.send1, s.recv1, s.asem.at[0], s.asem.at[1])
    kernel_quads(s, level, 1)
    ready("sens", "data")
    for c in range(s.sens.shape[0]):
        for h in range(2):
            s.sf[c, h] = folded(s, s.sens[c, h])
    wait_bytes(s.recv1.at[pl.ds(0, nf - 1)], s.asem.at[1])
    rows1 = (s.p0, s.p1, s.p2, s.p3)
    for t in range(2):
        place_rows(s.recv1, s.old, t, cols)
        spread_rows(s.old, t, rows1)
    fold_data(s, 0)
    for t in range(2):
        forward_rows(s.old, t, rows1)
    fold_data(s, 1)
    finish_rows(s.old, 0, rows1)
    for h in range(2):
        s.imf[0, h] = folded(s, s.old[0, h])
    sems = (s.s1, s.r1, s.s2, s.r2, s.s3, s.r3)
    coils = s.sens.shape[0]

    def pair(q, carry):
        run_pair(s, q // coils, q % coils)

        @pl.when(q == coils - 1)
        def _():
            unfold(s, 0)
            reduce_start(s.part, 0, s.xa, s.xd, sems)
            finish_rows(s.old, 1, rows1)
            for h in range(2):
                s.imf[1, h] = folded(s, s.old[1, h])

        @pl.when(q == coils)
        def _():
            reduce_forward(s.part, 0, s.xa, s.xsum, s.xs, sems)

        return carry

    lax.fori_loop(0, 2 * coils, pair, 0)
    unfold(s, 1)
    reduce_start(s.part, 1, s.xa, s.xd, sems)
    reduce_finish(s.part, 0, s.xd, s.xs, s.total, sems)
    send_columns(s.total, 0, s.rsend, s.rrecv, s.rsem, cols)
    reduce_forward(s.part, 1, s.xa, s.xsum, s.xs, sems)
    wait_bytes(s.rrecv.at[0, pl.ds(0, nf - 1)], s.rsem.at[1, 0])
    gradient_step(s.weights, s.rrecv, 0, s.grad)
    reduce_finish(s.part, 1, s.xd, s.xs, s.total, sems)
    send_columns(s.total, 1, s.rsend, s.rrecv, s.rsem, cols)
    wait_bytes(s.rrecv.at[1, pl.ds(0, nf - 1)], s.rsem.at[1, 1])
    gradient_step(s.weights, s.rrecv, 1, s.grad)
    for r in range(s.factors.shape[0]):
        s.factors[r] = s.factors[r] - STEP_SIZE * s.grad[r]
    share_images(s.weights, s.factors, s.send2, s.recv2, image, cols, s.bsem, (s.q0, s.q1, s.q2, s.q3), lambda: unpack_factors(s.factors, spatial_next))
    wait_bytes(s.weights.at[pl.ds(0, nf - 1)], s.wsem.at[0])
    wait_bytes(s.recv1.at[pl.ds(0, nf - 1)], s.asem.at[0])
    for t in range(2):
        wait_bytes(s.rrecv.at[t, pl.ds(0, nf - 1)], s.rsem.at[0, t])
        for way in range(2):
            for sem in (s.s1, s.s2, s.s3):
                wait_bytes(s.xa.at[t, way], sem.at[t, way])


def body(spatial, temporal, sensitivity, coil_data, kernel_index, kernel_level):
    size = sensitivity.shape[2]
    rank, _, rows_mine, cols = spatial.shape
    frames, coils = coil_data.shape[:2]
    nf = lax.axis_size("frame")
    padded = jnp.pad(spatial, ((0, 0), (0, 0), (0, 0), (0, 128 - cols)))
    weight = jnp.broadcast_to(temporal[:, :, None], temporal.shape + (128,))
    level = kernel_level / (4.0 * size * size)
    tables = make_tables(size)
    half = size // 2
    wide = tables["place"].shape[1] // 2
    rows = tables["f2c"].shape[0]
    slots = tables["mirror"].shape[1]
    chunks = slots // 128
    operands = dict(spatial=padded, index=kernel_index, sens=sensitivity, data=coil_data)
    operands.update({n: jnp.asarray(tables[n]) for n in TABLES})
    vm = pl.BlockSpec(memory_space=pltpu.VMEM)
    block = pltpu.VMEM((frames, 2, rows_mine, size), F32)
    dma = pltpu.SemaphoreType.DMA
    scratch = {n: pltpu.VMEM(x.shape, x.dtype) for n, x in operands.items()}
    scratch.update(
        kq=pltpu.VMEM((frames, 4, rows, slots), F32),
        sf=pltpu.VMEM((coils, 2, size, 2 * wide), F32),
        imf=pltpu.VMEM((frames, 2, size, 2 * wide), F32),
        res=pltpu.VMEM((frames, 2, size, 2 * wide), F32),
        lc=pltpu.VMEM((2, 4 * half, half), BF),
        ls=pltpu.VMEM((2, 4 * half, half), BF),
        ge=pltpu.VMEM((chunks, 3 * half, 512), BF),
        go=pltpu.VMEM((chunks, 3 * half, 512), BF),
        spa=pltpu.VMEM((chunks, rows, 512), F32),
        spb=pltpu.VMEM((chunks, rows, 512), F32),
        za=pltpu.VMEM((chunks, 3 * rows, 512), BF),
        zb=pltpu.VMEM((chunks, 3 * rows, 512), BF),
        lhc=pltpu.VMEM((4 * half, 3 * slots), BF),
        lhs=pltpu.VMEM((4 * half, 3 * slots), BF),
        oc=pltpu.VMEM((4 * half, half), F32),
        osn=pltpu.VMEM((4 * half, half), F32),
        part=pltpu.VMEM((frames, 2, size, size), F32),
        old=pltpu.VMEM((frames, 2, size, size), BF),
        weights=pltpu.VMEM((nf, frames, rank, 128), F32),
        factors=pltpu.VMEM((rank, 16, 128), F32),
        grad=pltpu.VMEM((rank, 16, 128), F32),
        send1=pltpu.VMEM((nf, frames, 16, 128), BF),
        recv1=pltpu.VMEM((nf, frames, 16, 128), BF),
        send2=pltpu.VMEM((nf, frames, 16, 128), BF),
        recv2=pltpu.VMEM((nf, frames, 16, 128), BF),
        rsend=pltpu.VMEM((frames, nf, 16, 128), F32),
        rrecv=pltpu.VMEM((frames, nf, 16, 128), F32),
        xa=block, xd=block, xsum=block, xs=block,
        total=pltpu.VMEM((frames, 2, rows_mine, -(-size // 128) * 128), F32),
        lsem=dma((len(LOCAL),)),
        wsem=dma((2,)), asem=dma((2,)), bsem=dma((2,)), rsem=dma((2, 2)),
        s1=dma((2, 2)), r1=dma((2, 2)), s2=dma((2, 2)), r2=dma((2, 2)), s3=dma((2, 2)), r3=dma((2, 2)),
    )
    for first in "pq":
        scratch.update({first + str(n): sem for n, sem in enumerate(row_sems())})
    return pl.pallas_call(
        whole_kernel,
        out_shape=(jax.ShapeDtypeStruct(spatial.shape, F32), jax.ShapeDtypeStruct((frames, 2, size, size), BF)),
        in_specs=[vm, pl.BlockSpec(memory_space=pltpu.SMEM)] + [pl.BlockSpec(memory_space=pl.ANY)] * len(LOCAL),
        out_specs=(vm, vm),
        scratch_shapes=scratch,
        compiler_params=pltpu.CompilerParams(vmem_limit_bytes=60 * 2**20, collective_id=0, has_side_effects=True),
    )(weight, level, *[operands[n] for n in LOCAL])


def solution(mesh):
    placed = (
        P(None, None, "coil", "frame"),
        P("frame", None),
        P("coil", None, None, None),
        P("frame", "coil", None, None, None),
        P("frame", None, None),
        P("frame", None),
    )
    return jax.shard_map(
        body,
        mesh=mesh,
        in_specs=placed,
        out_specs=(P(None, None, "coil", "frame"), P("frame", None, None, None)),
        check_vma=False,
    )
```

time: 129 us -> 109 us (0.84)
  Pallas kernels: 121 us -> 98.9 us
  local copies, waits for them, and re-layouts: 6.25 us -> 7.59 us
    pallas_call x3 -> x1, Pallas kernels: 121 us -> 98.9 us  [body(): pl.pallas_call(whole_kernel, out_shape=(jax.ShapeDtypeStruct(spatial.shap...]
    unnamed x6 -> x2, local copies, waits for them, and re-layouts: 4.58 us -> 3.39 us
where the time goes in v2:
time: 109 us; the launch traced here: 108 us
  Pallas kernels  98.9 us (91%)
  local copies, waits for them, and re-layouts  7.59 us (7%)
  other arithmetic  1.27 us (1%)
    pallas_call x1, Pallas kernels, body(): pl.pallas_call(whole_kernel, out_shape=(jax.ShapeDtypeStruct(spatial.shap...  98.9 us
    unnamed x2, local copies, waits for them, and re-layouts  3.39 us

profile of v2, /device:TPU:1, one launch (start us, length us, event | category | flops | bytes accessed | tf_op | source)
XLA Modules:
  0.0 108.4 jit_solution(6263939039968511002)
XLA Ops:
  0.6 1.3 %broadcast_multiply_fusion.level = f32[2,8]{1,0:T(2,128)} fusion(f32[2,8]{1,0:T(2,128)} %param.24), kind=kLoop, calls=%fused_computation | loop fusion | flops 16 | bytes 128 | tf_op jit(solution)/shard_map/div | solution.py:557
  1.9 1.3 %broadcast_in_dim.2.weight = f32[2,8,128]{2,1,0:T(8,128)} broadcast(f32[2,8]{1,0:T(2,128)} %param.20), dimensions={0,1} | broadcast | bytes 8256 | tf_op jit(solution)/shard_map/broadcast_in_dim | solution.py:556
  3.2 1.1 %copy.21 = f32[8,2,80,10]{3,2,1,0:T(8,128)S(1)} copy(f32[8,2,80,10]{2,1,3,0:T(2,128)} %param.19) | data formatting | bytes 102400 | tf_op args[0]
  4.4 0.9 pad.4.refs_0_
  5.3 98.9 %shard_map.194 = (f32[8,2,80,10]{3,2,1,0:T(8,128)}, bf16[2,2,320,320]{3,2,1,0:T(8,128)(2,1)}) custom-call(f32[2,8,128]{2,1,0:T(8,128)} %broadcast_in_dim.2.weight, f32[2,8]{1,0:T(2,128)} %broadcast_multiply_fusion.level, f32[8,2,80,128]{3,2,1,0:T(8,128)} %pad.4.refs_0_, s32[2,640,640]{2,1,0:T(8,128)} %refs_1_.1, bf16[2,2,320,320]{3,2,1,0:T(8,128)(2,1)} %refs_2_.1, ...), custom_call_target="tpu_custom_call" | custom-call | tf_op jit(solution)/shard_map/pallas_call | solution.py:606
  104.1 2.0 %copy.22 = f32[8,2,80,10]{2,1,3,0:T(2,128)} copy(f32[8,2,80,10]{3,2,1,0:T(8,128)} %get-tuple-element.2) | data formatting | bytes 102400 | tf_op jit(solution)/shard_map/pallas_call | solution.py:606
  106.1 2.2 %copy.24 = bf16[2,2,320,320]{3,2,1,0:T(8,128)(2,1)} copy(bf16[2,2,320,320]{3,2,1,0:T(8,128)(2,1)} %get-tuple-element.7) | data formatting | bytes 1638400

commit v3 on v2

--- a/solution.py
+++ b/solution.py
@@ -20,7 +20,7 @@
     return high, low
 
 
-def make_tables(size):
+def make_tables(size, blocks, cols):
     half = size // 2
     slots = -(-(size + 1) // 128) * 128
     rows = -(-(size + 1) // 16) * 16
@@ -57,10 +57,16 @@
     mirror[(2 * size - kk) % (2 * size), kk] = 1
     out["mirror"] = mirror.astype(ml_dtypes.bfloat16)
     out["mirror_rows"] = mirror.T[:rows].astype(ml_dtypes.bfloat16)
+    spread = np.zeros((32, 128))
+    for c in range(2):
+        for rb in range(blocks):
+            for j in range(cols):
+                spread[2 * j + c, (c * blocks + rb) * cols + j] = 1
+    out["spread"] = spread.astype(ml_dtypes.bfloat16)
     return out
 
 
-TABLES = ("f1c", "f1s", "f2c", "f2s", "i1c", "i1s", "i2c", "i2s", "place", "unplace", "flip", "mirror", "mirror_rows")
+TABLES = ("f1c", "f1s", "f2c", "f2s", "i1c", "i1s", "i2c", "i2s", "place", "unplace", "flip", "mirror", "mirror_rows", "spread")
 
 
 def mm(a, b):
@@ -76,14 +82,16 @@
 def kernel_quads(s, level, t):
     rows = s.f2c.shape[0]
     slots = s.mirror.shape[1]
+    size = 2 * s.flip.shape[0]
+    values = [level[t, m] * (0.25 / (size * size)) for m in range(level.shape[1])]
     ib = s.index[t].astype(F32).astype(BF)
     flipped = mm(ib, s.mirror[...]).astype(BF)
     low = mm(s.mirror_rows[...], jnp.concatenate([ib[:, :slots], flipped], axis=1))
     quads = (ib[:rows, :slots].astype(F32), flipped[:rows].astype(F32), low[:, :slots], low[:, slots:])
     for n, quad in enumerate(quads):
-        value = jnp.full(quad.shape, level[t, 0], F32)
-        for m in range(1, level.shape[1]):
-            value = jnp.where(quad > m - 0.5, level[t, m], value)
+        value = jnp.full(quad.shape, values[0], F32)
+        for m in range(1, len(values)):
+            value = jnp.where(quad > m - 0.5, values[m], value)
         s.kq[t, n] = value
 
 
@@ -153,6 +161,7 @@
     for j in range(chunks):
         s.spa[j] = mm(s.f2c[...], s.ge[j])
         s.spb[j] = mm(s.f2s[...], s.go[j])
+    for j in range(chunks):
         for r in range(0, rows, 16):
             rs = pl.ds(r, 16)
             aar, aai, abr, abi = (s.spa[j, rs, pl.ds(128 * m, 128)] for m in range(4))
@@ -173,6 +182,7 @@
                     dest[j, pl.ds(r, 16), lanes] = high
                     dest[j, pl.ds(rows + r, 16), lanes] = low
                     dest[j, pl.ds(2 * rows + r, 16), lanes] = high
+    for j in range(chunks):
         for n, (tab, src) in enumerate(((s.i1c, s.za), (s.i1s, s.zb))):
             high, low = split(mm(tab[...], src[j]))
             for m in range(4):
@@ -248,11 +258,11 @@
     pltpu.make_async_copy(ref, ref, sem).wait()
 
 
-def mix_and_send(weights, factors, send_buf, recv_buf, send_sem, recv_sem):
+def mix_and_send(weights, factors, t, send_buf, recv_buf, sems):
     frame, nf = lax.axis_index("frame"), lax.axis_size("frame")
     rank = factors.shape[0]
 
-    def piece(d, t):
+    def piece(d):
         total = weights[d, t, pl.ds(0, 1)] * factors[0]
         for r in range(1, rank):
             total += weights[d, t, pl.ds(r, 1)] * factors[r]
@@ -260,14 +270,16 @@
 
     def step(i, carry):
         d = lax.rem(frame + i, nf)
-        for t in range(2):
-            send_buf[d, t] = piece(d, t)
-        remote(send_buf.at[d], recv_buf.at[frame], send_sem, recv_sem, {"frame": d}).start()
+        send_buf[t, d] = piece(d)
+        remote(send_buf.at[t, d], recv_buf.at[t, frame], sems.at[0, t], sems.at[1, t], {"frame": d}).start()
         return carry
 
     lax.fori_loop(1, nf, step, 0)
-    for t in range(2):
-        recv_buf[frame, t] = piece(frame, t)
+    recv_buf[t, frame] = piece(frame)
+
+
+def wait_frames(buf, t, sem):
+    wait_bytes(buf.at[t, pl.ds(0, buf.shape[1] - 1)], sem)
 
 
 def place_rows(recv_buf, image, t, cols):
@@ -280,7 +292,7 @@
         for rb in range(blocks):
             tiles = [jnp.zeros((16, 128), F32) for _ in range(-(-size // 128))]
             for f in range(nf):
-                value = recv_buf[f, t].astype(F32)
+                value = recv_buf[t, f].astype(F32)
                 for tile, at, off, count in moves(f, cols, c * blocks + rb):
                     inside = (lane >= at) & (lane < at + count)
                     tiles[tile] = jnp.where(inside, roll(value, at - off), tiles[tile])
@@ -325,39 +337,75 @@
             wait_bytes(part, send.at[t, way, c])
 
 
-def share_images(weights, factors, send_buf, recv_buf, image, cols, a2a, rows_sems, between=None):
-    nf = lax.axis_size("frame")
-    mix_and_send(weights, factors, send_buf, recv_buf, a2a.at[0], a2a.at[1])
-    if between is not None:
-        between()
-    wait_bytes(recv_buf.at[pl.ds(0, nf - 1)], a2a.at[1])
-    for t in range(2):
-        place_rows(recv_buf, image, t, cols)
-        spread_rows(image, t, rows_sems)
-    for t in range(2):
-        forward_rows(image, t, rows_sems)
-    for t in range(2):
-        finish_rows(image, t, rows_sems)
-    wait_bytes(recv_buf.at[pl.ds(0, nf - 1)], a2a.at[0])
-
-
-def pack_factors(spatial, factors):
-    rank, _, rows, _ = spatial.shape
-    cols = 10
+def share_images(s, image, cols, sems, between):
+    for t in range(2):
+        mix_and_send(s.weights, s.factors, t, s.send2, s.recv2, s.bsem)
+    between()
+    for t in range(2):
+        wait_frames(s.recv2, t, s.bsem.at[1, t])
+        place_rows(s.recv2, image, t, cols)
+        spread_rows(image, t, sems)
+    for t in range(2):
+        forward_rows(image, t, sems)
+    for t in range(2):
+        finish_rows(image, t, sems)
+        wait_frames(s.send2, t, s.bsem.at[0, t])
+
+
+def thirds(x):
+    high, low = split(x)
+    rest = (x - high.astype(F32)) - low.astype(F32)
+    return high, low, rest.astype(BF)
+
+
+def group_mask(rb, blocks, cols):
     lane = lax.broadcasted_iota(jnp.int32, (16, 128), 1)
+    first, second = rb * cols, (blocks + rb) * cols
+    return ((lane >= first) & (lane < first + cols)) | ((lane >= second) & (lane < second + cols))
+
+
+def pack_factors(s):
+    rank, cols, _, rows = s.spatial.shape
     blocks = rows // 16
-
-    def one(r, carry):
+    s.flat[...] = jnp.zeros(s.flat.shape, F32)
+    for r in range(rank):
+        for j in range(cols):
+            s.flat[pl.ds(2 * j, 2), pl.ds(128 * r, rows)] = s.spatial[r, j]
+    turned = sum(lax.dot_general(x, s.spread[...], (((0,), (0,)), ((), ())), preferred_element_type=F32) for x in thirds(s.flat[...]))
+    for r in range(rank):
         total = jnp.zeros((16, 128), F32)
-        for c in range(2):
-            for rb in range(blocks):
-                off = (c * blocks + rb) * cols
-                inside = (lane >= off) & (lane < off + cols)
-                total = jnp.where(inside, roll(spatial[r, c, pl.ds(16 * rb, 16)], off), total)
-        factors[r] = total
+        for rb in range(blocks):
+            at = 128 * r + 16 * rb
+            total = jnp.where(group_mask(rb, blocks, cols), turned[at:at + 16], total)
+        s.factors[r] = total
+
+
+def unpack_factors(s, spatial_next):
+    rank, cols, _, rows = spatial_next.shape
+    blocks = rows // 16
+    s.wide[...] = jnp.zeros(s.wide.shape, F32)
+    for r in range(rank):
+        value = s.factors[r]
+        for rb in range(blocks):
+            s.wide[pl.ds(128 * r + 16 * rb, 16)] = jnp.where(group_mask(rb, blocks, cols), value, 0.0)
+    turned = sum(lax.dot_general(s.spread[...], x, (((1,), (1,)), ((), ())), preferred_element_type=F32) for x in thirds(s.wide[...]))
+    for r in range(rank):
+        for j in range(cols):
+            spatial_next[r, j] = turned[2 * j:2 * j + 2, 128 * r:128 * r + rows]
+
+
+def widen_weights(s):
+    nf, frames, rank = s.raw.shape
+    one = lax.broadcasted_iota(jnp.int32, (rank, rank), 0) == lax.broadcasted_iota(jnp.int32, (rank, rank), 1)
+
+    def step(d, carry):
+        for t in range(frames):
+            row = jnp.broadcast_to(s.raw[d, pl.ds(t, 1)], (rank, rank))
+            column = jnp.sum(jnp.where(one, row, 0.0), axis=1, keepdims=True)
+            s.weights[d, t] = jnp.broadcast_to(column, (rank, 128))
         return carry
 
-    lax.fori_loop(0, rank, one, 0)
+    lax.fori_loop(0, nf, step, 0, unroll=8)
 
 
 def row_sems():
@@ -441,20 +489,6 @@
         grad[r] = acc[r] if t == 0 else grad[r] + acc[r]
 
 
-def unpack_factors(factors, spatial):
-    rank, _, rows, cols = spatial.shape
-    blocks = rows // 16
-
-    def one(r, carry):
-        value = factors[r]
-        for c in range(2):
-            for rb in range(blocks):
-                spatial[r, c, pl.ds(16 * rb, 16)] = roll(value, -(c * blocks + rb) * cols)[:, :cols]
-        return carry
-
-    lax.fori_loop(0, rank, one, 0)
-
-
 LOCAL = ("spatial", "index", "sens", "data") + TABLES
 
 
@@ -462,7 +496,7 @@
     s = types.SimpleNamespace(**scratch)
     sources, (spatial_next, image) = refs[:len(LOCAL)], refs[len(LOCAL):]
     frame, nf = lax.axis_index("frame"), lax.axis_size("frame")
-    cols = spatial_next.shape[3]
+    cols = spatial_next.shape[1]
     copies = {}
     for n, (name, source) in enumerate(zip(LOCAL, sources)):
         copies[name] = pltpu.make_async_copy(source, scratch[name], s.lsem.at[n])
@@ -475,25 +509,27 @@
     enter(None)
 
     def exchange(i, carry):
-        remote(weight, s.weights.at[frame], s.wsem.at[0], s.wsem.at[1], {"frame": lax.rem(frame + i, nf)}).start()
+        remote(weight, s.raw.at[frame], s.wsem.at[0], s.wsem.at[1], {"frame": lax.rem(frame + i, nf)}).start()
         return carry
 
     lax.fori_loop(1, nf, exchange, 0)
-    s.weights[frame] = weight[...]
-    ready("spatial")
-    pack_factors(s.spatial, s.factors)
-    ready("index", *TABLES)
+    s.raw[frame] = weight[...]
+    ready("spatial", "spread")
+    pack_factors(s)
+    ready("index", *(n for n in TABLES if n != "spread"))
     kernel_quads(s, level, 0)
-    wait_bytes(s.weights.at[pl.ds(0, nf - 1)], s.wsem.at[1])
-    mix_and_send(s.weights, s.factors, s.send1, s.recv1, s.asem.at[0], s.asem.at[1])
+    wait_bytes(s.raw.at[pl.ds(0, nf - 1)], s.wsem.at[1])
+    widen_weights(s)
+    for t in range(2):
+        mix_and_send(s.weights, s.factors, t, s.send1, s.recv1, s.asem)
     kernel_quads(s, level, 1)
     ready("sens", "data")
     for c in range(s.sens.shape[0]):
         for h in range(2):
             s.sf[c, h] = folded(s, s.sens[c, h])
-    wait_bytes(s.recv1.at[pl.ds(0, nf - 1)], s.asem.at[1])
     rows1 = (s.p0, s.p1, s.p2, s.p3)
     for t in range(2):
+        wait_frames(s.recv1, t, s.asem.at[1, t])
         place_rows(s.recv1, s.old, t, cols)
         spread_rows(s.old, t, rows1)
     fold_data(s, 0)
@@ -537,9 +573,10 @@
     gradient_step(s.weights, s.rrecv, 1, s.grad)
     for r in range(s.factors.shape[0]):
         s.factors[r] = s.factors[r] - STEP_SIZE * s.grad[r]
-    share_images(s.weights, s.factors, s.send2, s.recv2, image, cols, s.bsem, (s.q0, s.q1, s.q2, s.q3), lambda: unpack_factors(s.factors, spatial_next))
-    wait_bytes(s.weights.at[pl.ds(0, nf - 1)], s.wsem.at[0])
-    wait_bytes(s.recv1.at[pl.ds(0, nf - 1)], s.asem.at[0])
+    share_images(s, image, cols, (s.q0, s.q1, s.q2, s.q3), lambda: unpack_factors(s, spatial_next))
+    wait_bytes(s.raw.at[pl.ds(0, nf - 1)], s.wsem.at[0])
+    for t in range(2):
+        wait_frames(s.send1, t, s.asem.at[0, t])
     for t in range(2):
         wait_bytes(s.rrecv.at[t, pl.ds(0, nf - 1)], s.rsem.at[0, t])
         for way in range(2):
@@ -552,16 +589,13 @@
     rank, _, rows_mine, cols = spatial.shape
     frames, coils = coil_data.shape[:2]
     nf = lax.axis_size("frame")
-    padded = jnp.pad(spatial, ((0, 0), (0, 0), (0, 0), (0, 128 - cols)))
-    weight = jnp.broadcast_to(temporal[:, :, None], temporal.shape + (128,))
-    level = kernel_level / (4.0 * size * size)
-    tables = make_tables(size)
+    tables = make_tables(size, rows_mine // 16, cols)
     half = size // 2
     wide = tables["place"].shape[1] // 2
     rows = tables["f2c"].shape[0]
     slots = tables["mirror"].shape[1]
     chunks = slots // 128
-    operands = dict(spatial=padded, index=kernel_index, sens=sensitivity, data=coil_data)
+    operands = dict(spatial=spatial.transpose(0, 3, 1, 2), index=kernel_index, sens=sensitivity, data=coil_data)
     operands.update({n: jnp.asarray(tables[n]) for n in TABLES})
     vm = pl.BlockSpec(memory_space=pltpu.VMEM)
     block = pltpu.VMEM((frames, 2, rows_mine, size), F32)
@@ -586,31 +620,35 @@
         osn=pltpu.VMEM((4 * half, half), F32),
         part=pltpu.VMEM((frames, 2, size, size), F32),
         old=pltpu.VMEM((frames, 2, size, size), BF),
+        raw=pltpu.VMEM((nf, frames, rank), F32),
+        flat=pltpu.VMEM((32, 128 * rank), F32),
+        wide=pltpu.VMEM((128 * rank, 128), F32),
         weights=pltpu.VMEM((nf, frames, rank, 128), F32),
         factors=pltpu.VMEM((rank, 16, 128), F32),
         grad=pltpu.VMEM((rank, 16, 128), F32),
-        send1=pltpu.VMEM((nf, frames, 16, 128), BF),
-        recv1=pltpu.VMEM((nf, frames, 16, 128), BF),
-        send2=pltpu.VMEM((nf, frames, 16, 128), BF),
-        recv2=pltpu.VMEM((nf, frames, 16, 128), BF),
+        send1=pltpu.VMEM((frames, nf, 16, 128), BF),
+        recv1=pltpu.VMEM((frames, nf, 16, 128), BF),
+        send2=pltpu.VMEM((frames, nf, 16, 128), BF),
+        recv2=pltpu.VMEM((frames, nf, 16, 128), BF),
         rsend=pltpu.VMEM((frames, nf, 16, 128), F32),
         rrecv=pltpu.VMEM((frames, nf, 16, 128), F32),
         xa=block, xd=block, xsum=block, xs=block,
         total=pltpu.VMEM((frames, 2, rows_mine, -(-size // 128) * 128), F32),
         lsem=dma((len(LOCAL),)),
-        wsem=dma((2,)), asem=dma((2,)), bsem=dma((2,)), rsem=dma((2, 2)),
+        wsem=dma((2,)), asem=dma((2, 2)), bsem=dma((2, 2)), rsem=dma((2, 2)),
         s1=dma((2, 2)), r1=dma((2, 2)), s2=dma((2, 2)), r2=dma((2, 2)), s3=dma((2, 2)), r3=dma((2, 2)),
     )
     for first in "pq":
         scratch.update({first + str(n): sem for n, sem in enumerate(row_sems())})
-    return pl.pallas_call(
+    result, images = pl.pallas_call(
         whole_kernel,
-        out_shape=(jax.ShapeDtypeStruct(spatial.shape, F32), jax.ShapeDtypeStruct((frames, 2, size, size), BF)),
+        out_shape=(jax.ShapeDtypeStruct((rank, cols, 2, rows_mine), F32), jax.ShapeDtypeStruct((frames, 2, size, size), BF)),
         in_specs=[vm, pl.BlockSpec(memory_space=pltpu.SMEM)] + [pl.BlockSpec(memory_space=pl.ANY)] * len(LOCAL),
         out_specs=(vm, vm),
         scratch_shapes=scratch,
         compiler_params=pltpu.CompilerParams(vmem_limit_bytes=60 * 2**20, collective_id=0, has_side_effects=True),
-    )(weight, level, *[operands[n] for n in LOCAL])
+    )(temporal, kernel_level, *[operands[n] for n in LOCAL])
+    return result.transpose(0, 2, 3, 1), images
 
 
 def solution(mesh):

time: 109 us -> 97.8 us (0.90)
  Pallas kernels: 98.9 us -> 93.1 us
  local copies, waits for them, and re-layouts: 7.59 us -> 3.77 us
  other arithmetic: 1.27 us -> 0 us
    pallas_call x1, Pallas kernels: 98.9 us -> 93.1 us  [body(): pl.pallas_call(whole_kernel, out_shape=(jax.ShapeDtypeStruct((rank, cols,...]
    pallas_call x1 -> x0, local copies, waits for them, and re-layouts: 1.97 us -> none  [body(): pl.pallas_call(whole_kernel, out_shape=(jax.ShapeDtypeStruct(spatial.shap...]
    broadcast_in_dim x1 -> x0, local copies, waits for them, and re-layouts: 1.35 us -> none  [body(): weight = jnp.broadcast_to(temporal[:, :, None], temporal.shape + (128,))]
    div x1 -> x0, other arithmetic: 1.27 us -> none  [body(): level = kernel_level / (4.0 * size * size)]
where the time goes in v3:
time: 97.8 us; the launch traced here: 97.6 us
  Pallas kernels  93.1 us (95%)
  local copies, waits for them, and re-layouts  3.77 us (4%)
    pallas_call x1, Pallas kernels, body(): pl.pallas_call(whole_kernel, out_shape=(jax.ShapeDtypeStruct((rank, cols,...  93.1 us
    unnamed x2, local copies, waits for them, and re-layouts  3.77 us

profile of v3, /device:TPU:1, one launch (start us, length us, event | category | flops | bytes accessed | tf_op | source)
XLA Modules:
  0.0 97.6 jit_solution(8243587411273709576)
XLA Ops:
  0.6 93.1 %shard_map.203 = (f32[8,10,2,80]{3,2,1,0:T(2,128)}, bf16[2,2,320,320]{3,2,1,0:T(8,128)(2,1)}) custom-call(f32[2,8]{1,0:T(2,128)} %weight.1, f32[2,8]{1,0:T(2,128)} %level.1, f32[8,10,2,80]{3,2,1,0:T(2,128)} %bitcast.2, s32[2,640,640]{2,1,0:T(8,128)} %refs_1_.1, bf16[2,2,320,320]{3,2,1,0:T(8,128)(2,1)} %refs_2_.1, bf16[2,2,2,320,320]{4,3,2,1,0:T(8,128)(2,1)} %refs_3_.1, ...), custom_call_target="tpu_custom_call" | custom-call | tf_op jit(solution)/shard_map/pallas_call | solution.py:643
  93.8 1.5 %copy.24 = f32[8,2,80,10]{2,1,3,0:T(2,128)} copy(f32[8,2,80,10]{2,1,3,0:T(2,128)} %bitcast.3) | data formatting | bytes 102400
  95.3 2.2 %copy.25 = bf16[2,2,320,320]{3,2,1,0:T(8,128)(2,1)} copy(bf16[2,2,320,320]{3,2,1,0:T(8,128)(2,1)} %get-tuple-element.9) | data formatting | bytes 1638400

commit v4 on v3

--- a/solution.py
+++ b/solution.py
@@ -148,7 +148,8 @@
                 s.ls[0, pl.ds(at, 16)] = hs
                 s.ls[1, pl.ds(at, 16)] = ws
     for n, (lref, tab) in enumerate(((s.lc, s.f1c), (s.ls, s.f1s))):
-        first = mm(lref[0], tab[:, :slots]) + mm(lref[0], tab[:, slots:]) + mm(lref[1], tab[:, :slots])
+        both = mm(lref[0], tab[...])
+        first = both[:, :slots] + both[:, slots:] + mm(lref[1], tab[:, :slots])
         for k, dest in enumerate((s.ge, s.go)):
             for h in range(2):
                 part = first[(2 * k + h) * half:(2 * k + h + 1) * half]
@@ -158,14 +159,13 @@
                     dest[j, pl.ds(0, half), lanes] = high[:, j * 128:(j + 1) * 128]
                     dest[j, pl.ds(half, half), lanes] = low[:, j * 128:(j + 1) * 128]
                     dest[j, pl.ds(2 * half, half), lanes] = high[:, j * 128:(j + 1) * 128]
-    for j in range(chunks):
-        s.spa[j] = mm(s.f2c[...], s.ge[j])
-        s.spb[j] = mm(s.f2s[...], s.go[j])
+    even = [mm(s.f2c[...], s.ge[j]) for j in range(chunks)]
+    odd = [mm(s.f2s[...], s.go[j]) for j in range(chunks)]
     for j in range(chunks):
         for r in range(0, rows, 16):
             rs = pl.ds(r, 16)
-            aar, aai, abr, abi = (s.spa[j, rs, pl.ds(128 * m, 128)] for m in range(4))
-            bar, bai, bbr, bbi = (s.spb[j, rs, pl.ds(128 * m, 128)] for m in range(4))
+            aar, aai, abr, abi = (even[j][r:r + 16, 128 * m:128 * m + 128] for m in range(4))
+            bar, bai, bbr, bbi = (odd[j][r:r + 16, 128 * m:128 * m + 128] for m in range(4))
             kpp, kpm, kmp, kmm = (s.kq[t, m, rs, pl.ds(128 * j, 128)] for m in range(4))
             ur, ui, vr, vi = aar - bbr, aai - bbi, aar + bbr, aai + bbi
             wr, wi, qr, qi = abr + bar, abi + bai, abr - bar, abi - bai
@@ -528,13 +528,14 @@
         for h in range(2):
             s.sf[c, h] = folded(s, s.sens[c, h])
     rows1 = (s.p0, s.p1, s.p2, s.p3)
-    for t in range(2):
-        wait_frames(s.recv1, t, s.asem.at[1, t])
-        place_rows(s.recv1, s.old, t, cols)
-        spread_rows(s.old, t, rows1)
+    wait_frames(s.recv1, 0, s.asem.at[1, 0])
+    place_rows(s.recv1, s.old, 0, cols)
+    spread_rows(s.old, 0, rows1)
+    wait_frames(s.recv1, 1, s.asem.at[1, 1])
+    place_rows(s.recv1, s.old, 1, cols)
     fold_data(s, 0)
-    for t in range(2):
-        forward_rows(s.old, t, rows1)
+    forward_rows(s.old, 0, rows1)
+    spread_rows(s.old, 1, rows1)
     fold_data(s, 1)
     finish_rows(s.old, 0, rows1)
     for h in range(2):
@@ -544,6 +545,10 @@
 
     def pair(q, carry):
         run_pair(s, q // coils, q % coils)
+
+        @pl.when(q == 0)
+        def _():
+            forward_rows(s.old, 1, rows1)
 
         @pl.when(q == coils - 1)
         def _():
@@ -582,6 +587,29 @@
         for way in range(2):
             for sem in (s.s1, s.s2, s.s3):
                 wait_bytes(s.xa.at[t, way], sem.at[t, way])
+
+
+def settle_kernel(result, images, result_out, images_out, sems):
+    copies = [pltpu.make_async_copy(result, result_out, sems.at[0])]
+    frames, parts = images.shape[:2]
+    for t in range(frames):
+        for h in range(parts):
+            copies.append(pltpu.make_async_copy(images.at[t, h], images_out.at[t, h], sems.at[1 + parts * t + h]))
+    for copy in copies:
+        copy.start()
+    for copy in copies:
+        copy.wait()
+
+
+def settle(result, images):
+    anywhere = pl.BlockSpec(memory_space=pl.ANY)
+    return pl.pallas_call(
+        settle_kernel,
+        out_shape=(jax.ShapeDtypeStruct(result.shape, result.dtype), jax.ShapeDtypeStruct(images.shape, images.dtype)),
+        in_specs=[anywhere, anywhere],
+        out_specs=(anywhere, anywhere),
+        scratch_shapes=[pltpu.SemaphoreType.DMA((1 + images.shape[0] * images.shape[1],))],
+    )(result, images)
 
 
 def body(spatial, temporal, sensitivity, coil_data, kernel_index, kernel_level):
@@ -610,8 +638,6 @@
         ls=pltpu.VMEM((2, 4 * half, half), BF),
         ge=pltpu.VMEM((chunks, 3 * half, 512), BF),
         go=pltpu.VMEM((chunks, 3 * half, 512), BF),
-        spa=pltpu.VMEM((chunks, rows, 512), F32),
-        spb=pltpu.VMEM((chunks, rows, 512), F32),
         za=pltpu.VMEM((chunks, 3 * rows, 512), BF),
         zb=pltpu.VMEM((chunks, 3 * rows, 512), BF),
         lhc=pltpu.VMEM((4 * half, 3 * slots), BF),
@@ -640,14 +666,14 @@
     )
     for first in "pq":
         scratch.update({first + str(n): sem for n, sem in enumerate(row_sems())})
-    result, images = pl.pallas_call(
+    result, images = settle(*pl.pallas_call(
         whole_kernel,
         out_shape=(jax.ShapeDtypeStruct((rank, cols, 2, rows_mine), F32), jax.ShapeDtypeStruct((frames, 2, size, size), BF)),
         in_specs=[vm, pl.BlockSpec(memory_space=pltpu.SMEM)] + [pl.BlockSpec(memory_space=pl.ANY)] * len(LOCAL),
         out_specs=(vm, vm),
         scratch_shapes=scratch,
         compiler_params=pltpu.CompilerParams(vmem_limit_bytes=60 * 2**20, collective_id=0, has_side_effects=True),
-    )(temporal, kernel_level, *[operands[n] for n in LOCAL])
+    )(temporal, kernel_level, *[operands[n] for n in LOCAL]))
     return result.transpose(0, 2, 3, 1), images
 
 

time: 97.8 us -> 126 us (1.29)
  Pallas kernels: 93.1 us -> 125 us
  local copies, waits for them, and re-layouts: 3.77 us -> 0 us
    pallas_call x0 -> x1, Pallas kernels: none -> 33.4 us  [settle(): pl.pallas_call(settle_kernel, out_shape=(jax.ShapeDtypeStruct(result.shap...]
    unnamed x2 -> x0, local copies, waits for them, and re-layouts: 3.77 us -> none
where the time goes in v4:
time: 126 us
  Pallas kernels  125 us (99%)
    pallas_call x1, Pallas kernels, body(): pl.pallas_call(whole_kernel, out_shape=(jax.ShapeDtypeStruct((rank, cols,...  92 us
    pallas_call x1, Pallas kernels, settle(): pl.pallas_call(settle_kernel, out_shape=(jax.ShapeDtypeStruct(result.shap...  33.4 us

profile of v4, /device:TPU:1, one launch (start us, length us, event | category | flops | bytes accessed | tf_op | source)
XLA Modules:
  0.0 126.2 jit_solution(13010332398601117414)
XLA Ops:
  0.6 92.0 %shard_map.203 = (f32[8,10,2,80]{3,2,1,0:T(2,128)}, bf16[2,2,320,320]{3,2,1,0:T(8,128)(2,1)}) custom-call(f32[2,8]{1,0:T(2,128)} %weight.1, f32[2,8]{1,0:T(2,128)} %level.1, f32[8,10,2,80]{3,2,1,0:T(2,128)} %bitcast.2, s32[2,640,640]{2,1,0:T(8,128)} %refs_1_.1, bf16[2,2,320,320]{3,2,1,0:T(8,128)(2,1)} %refs_2_.1, bf16[2,2,2,320,320]{4,3,2,1,0:T(8,128)(2,1)} %refs_3_.1, ...), custom_call_target="tpu_custom_call" | custom-call | tf_op jit(solution)/shard_map/pallas_call | solution.py:669
  92.6 33.4 %shard_map.204 = (f32[8,10,2,80]{3,2,1,0:T(2,128)}, bf16[2,2,320,320]{3,2,1,0:T(8,128)(2,1)}) custom-call(f32[8,10,2,80]{3,2,1,0:T(2,128)} %get-tuple-element.6.result, bf16[2,2,320,320]{3,2,1,0:T(8,128)(2,1)} %get-tuple-element.7.images), custom_call_target="tpu_custom_call" | custom-call | tf_op jit(solution)/shard_map/pallas_call | solution.py:606

commit v5 on v4

--- a/solution.py
+++ b/solution.py
@@ -122,12 +122,9 @@
         s.part[t, h, pl.ds(0, half)] = mm(s.flip[...], high) + mm(s.flip[...], low)
 
 
-def run_pair(s, t, c):
+def fold_pair(s, t, c):
     half = s.flip.shape[0]
     wide = s.place.shape[1] // 2
-    rows = s.f2c.shape[0]
-    slots = s.mirror.shape[1]
-    chunks = slots // 128
     for r in range(0, half, 16):
         parts = {}
         for a, row in (("R", r), ("L", half + r)):
@@ -147,6 +144,14 @@
                 s.lc[1, pl.ds(at, 16)] = wc
                 s.ls[0, pl.ds(at, 16)] = hs
                 s.ls[1, pl.ds(at, 16)] = ws
+
+
+def run_pair(s, t, c):
+    half = s.flip.shape[0]
+    wide = s.place.shape[1] // 2
+    rows = s.f2c.shape[0]
+    slots = s.mirror.shape[1]
+    chunks = slots // 128
     for n, (lref, tab) in enumerate(((s.lc, s.f1c), (s.ls, s.f1s))):
         both = mm(lref[0], tab[...])
         first = both[:, :slots] + both[:, slots:] + mm(lref[1], tab[:, :slots])
@@ -190,6 +195,8 @@
                 rs = pl.ds((2 * n + m % 2) * half, half)
                 for place_at, value in enumerate((high, low, high)):
                     dest[rs, pl.ds(j * 384 + place_at * 128, 128)] = value[:, 128 * m:128 * (m + 1)]
+    following = lax.rem(t * s.sens.shape[0] + c + 1, s.res.shape[0] * s.sens.shape[0])
+    fold_pair(s, following // s.sens.shape[0], following % s.sens.shape[0])
     s.oc[...] = mm(s.lhc[...], s.i2c[...])
     s.osn[...] = mm(s.lhs[...], s.i2s[...])
     for r in range(0, half, 16):
@@ -543,7 +550,15 @@
     sems = (s.s1, s.r1, s.s2, s.r2, s.s3, s.r3)
     coils = s.sens.shape[0]
 
+    fold_pair(s, 0, 0)
+
     def pair(q, carry):
+        @pl.when(q == coils - 1)
+        def _():
+            finish_rows(s.old, 1, rows1)
+            for h in range(2):
+                s.imf[1, h] = folded(s, s.old[1, h])
+
         run_pair(s, q // coils, q % coils)
 
         @pl.when(q == 0)
@@ -554,9 +569,6 @@
         def _():
             unfold(s, 0)
             reduce_start(s.part, 0, s.xa, s.xd, sems)
-            finish_rows(s.old, 1, rows1)
-            for h in range(2):
-                s.imf[1, h] = folded(s, s.old[1, h])
 
         @pl.when(q == coils)
         def _():
@@ -589,15 +601,18 @@
                 wait_bytes(s.xa.at[t, way], sem.at[t, way])
 
 
-def settle_kernel(result, images, result_out, images_out, sems):
-    copies = [pltpu.make_async_copy(result, result_out, sems.at[0])]
+def settle_kernel(result, images, result_out, images_out, small, large, sems):
     frames, parts = images.shape[:2]
-    for t in range(frames):
-        for h in range(parts):
-            copies.append(pltpu.make_async_copy(images.at[t, h], images_out.at[t, h], sems.at[1 + parts * t + h]))
-    for copy in copies:
+    legs = [(result, small, result_out)]
+    legs += [(images.at[t, h], large.at[t, h], images_out.at[t, h]) for t in range(frames) for h in range(parts)]
+    into = [pltpu.make_async_copy(src, mid, sems.at[0, n]) for n, (src, mid, _) in enumerate(legs)]
+    out = [pltpu.make_async_copy(mid, dst, sems.at[1, n]) for n, (_, mid, dst) in enumerate(legs)]
+    for copy in into:
         copy.start()
-    for copy in copies:
+    for first, second in zip(into, out):
+        first.wait()
+        second.start()
+    for copy in out:
         copy.wait()
 
 
@@ -608,7 +623,11 @@
         out_shape=(jax.ShapeDtypeStruct(result.shape, result.dtype), jax.ShapeDtypeStruct(images.shape, images.dtype)),
         in_specs=[anywhere, anywhere],
         out_specs=(anywhere, anywhere),
-        scratch_shapes=[pltpu.SemaphoreType.DMA((1 + images.shape[0] * images.shape[1],))],
+        scratch_shapes=[
+            pltpu.VMEM(result.shape, result.dtype),
+            pltpu.VMEM(images.shape, images.dtype),
+            pltpu.SemaphoreType.DMA((2, 1 + images.shape[0] * images.shape[1])),
+        ],
     )(result, images)
 
 

time: 126 us -> 98.6 us (0.78)
  Pallas kernels: 125 us -> 97.6 us
    pallas_call x1, Pallas kernels: 33.4 us -> 2.09 us  [settle(): pl.pallas_call(settle_kernel, out_shape=(jax.ShapeDtypeStruct(result.shap...]
    pallas_call x1, Pallas kernels: 92 us -> 95.6 us  [body(): pl.pallas_call(whole_kernel, out_shape=(jax.ShapeDtypeStruct((rank, cols,...]
where the time goes in v5:
time: 98.6 us; the launch traced here: 98.4 us
  Pallas kernels  97.6 us (99%)
    pallas_call x1, Pallas kernels, body(): pl.pallas_call(whole_kernel, out_shape=(jax.ShapeDtypeStruct((rank, cols,...  95.6 us
    pallas_call x1, Pallas kernels, settle(): pl.pallas_call(settle_kernel, out_shape=(jax.ShapeDtypeStruct(result.shap...  2.09 us

profile of v5, /device:TPU:1, one launch (start us, length us, event | category | flops | bytes accessed | tf_op | source)
XLA Modules:
  0.0 98.4 jit_solution(5670953919128673425)
XLA Ops:
  0.6 95.6 %shard_map.203 = (f32[8,10,2,80]{3,2,1,0:T(2,128)}, bf16[2,2,320,320]{3,2,1,0:T(8,128)(2,1)}) custom-call(f32[2,8]{1,0:T(2,128)} %weight.1, f32[2,8]{1,0:T(2,128)} %level.1, f32[8,10,2,80]{3,2,1,0:T(2,128)} %bitcast.2, s32[2,640,640]{2,1,0:T(8,128)} %refs_1_.1, bf16[2,2,320,320]{3,2,1,0:T(8,128)(2,1)} %refs_2_.1, bf16[2,2,2,320,320]{4,3,2,1,0:T(8,128)(2,1)} %refs_3_.1, ...), custom_call_target="tpu_custom_call" | custom-call | tf_op jit(solution)/shard_map/pallas_call | solution.py:688
  96.2 2.1 %shard_map.204 = (f32[8,10,2,80]{3,2,1,0:T(2,128)}, bf16[2,2,320,320]{3,2,1,0:T(8,128)(2,1)}) custom-call(f32[8,10,2,80]{3,2,1,0:T(2,128)} %get-tuple-element.6.result, bf16[2,2,320,320]{3,2,1,0:T(8,128)(2,1)} %get-tuple-element.7.images), custom_call_target="tpu_custom_call" | custom-call | tf_op jit(solution)/shard_map/pallas_call | solution.py:621

commit v6 on v5

--- a/solution.py
+++ b/solution.py
@@ -122,9 +122,12 @@
         s.part[t, h, pl.ds(0, half)] = mm(s.flip[...], high) + mm(s.flip[...], low)
 
 
-def fold_pair(s, t, c):
+def run_pair(s, t, c):
     half = s.flip.shape[0]
     wide = s.place.shape[1] // 2
+    rows = s.f2c.shape[0]
+    slots = s.mirror.shape[1]
+    chunks = slots // 128
     for r in range(0, half, 16):
         parts = {}
         for a, row in (("R", r), ("L", half + r)):
@@ -144,14 +147,6 @@
                 s.lc[1, pl.ds(at, 16)] = wc
                 s.ls[0, pl.ds(at, 16)] = hs
                 s.ls[1, pl.ds(at, 16)] = ws
-
-
-def run_pair(s, t, c):
-    half = s.flip.shape[0]
-    wide = s.place.shape[1] // 2
-    rows = s.f2c.shape[0]
-    slots = s.mirror.shape[1]
-    chunks = slots // 128
     for n, (lref, tab) in enumerate(((s.lc, s.f1c), (s.ls, s.f1s))):
         both = mm(lref[0], tab[...])
         first = both[:, :slots] + both[:, slots:] + mm(lref[1], tab[:, :slots])
@@ -195,8 +190,6 @@
                 rs = pl.ds((2 * n + m % 2) * half, half)
                 for place_at, value in enumerate((high, low, high)):
                     dest[rs, pl.ds(j * 384 + place_at * 128, 128)] = value[:, 128 * m:128 * (m + 1)]
-    following = lax.rem(t * s.sens.shape[0] + c + 1, s.res.shape[0] * s.sens.shape[0])
-    fold_pair(s, following // s.sens.shape[0], following % s.sens.shape[0])
     s.oc[...] = mm(s.lhc[...], s.i2c[...])
     s.osn[...] = mm(s.lhs[...], s.i2s[...])
     for r in range(0, half, 16):
@@ -496,7 +489,7 @@
         grad[r] = acc[r] if t == 0 else grad[r] + acc[r]
 
 
-LOCAL = ("spatial", "index", "sens", "data") + TABLES
+LOCAL = ("spatial", "spread", "index", "sens", "data") + TABLES[:-1]
 
 
 def whole_kernel(weight, level, *refs, **scratch):
@@ -523,13 +516,12 @@
     s.raw[frame] = weight[...]
     ready("spatial", "spread")
     pack_factors(s)
-    ready("index", *(n for n in TABLES if n != "spread"))
-    kernel_quads(s, level, 0)
     wait_bytes(s.raw.at[pl.ds(0, nf - 1)], s.wsem.at[1])
     widen_weights(s)
     for t in range(2):
         mix_and_send(s.weights, s.factors, t, s.send1, s.recv1, s.asem)
-    kernel_quads(s, level, 1)
+    ready("index", *TABLES[:-1])
+    kernel_quads(s, level, 0)
     ready("sens", "data")
     for c in range(s.sens.shape[0]):
         for h in range(2):
@@ -540,9 +532,10 @@
     spread_rows(s.old, 0, rows1)
     wait_frames(s.recv1, 1, s.asem.at[1, 1])
     place_rows(s.recv1, s.old, 1, cols)
-    fold_data(s, 0)
+    kernel_quads(s, level, 1)
     forward_rows(s.old, 0, rows1)
     spread_rows(s.old, 1, rows1)
+    fold_data(s, 0)
     fold_data(s, 1)
     finish_rows(s.old, 0, rows1)
     for h in range(2):
@@ -550,15 +543,7 @@
     sems = (s.s1, s.r1, s.s2, s.r2, s.s3, s.r3)
     coils = s.sens.shape[0]
 
-    fold_pair(s, 0, 0)
-
     def pair(q, carry):
-        @pl.when(q == coils - 1)
-        def _():
-            finish_rows(s.old, 1, rows1)
-            for h in range(2):
-                s.imf[1, h] = folded(s, s.old[1, h])
-
         run_pair(s, q // coils, q % coils)
 
         @pl.when(q == 0)
@@ -569,6 +554,9 @@
         def _():
             unfold(s, 0)
             reduce_start(s.part, 0, s.xa, s.xd, sems)
+            finish_rows(s.old, 1, rows1)
+            for h in range(2):
+                s.imf[1, h] = folded(s, s.old[1, h])
 
         @pl.when(q == coils)
         def _():

time: 98.6 us -> 95.1 us (0.965)
  Pallas kernels: 97.6 us -> 94.2 us
    pallas_call x1, Pallas kernels: 95.6 us -> 92.1 us  [body(): pl.pallas_call(whole_kernel, out_shape=(jax.ShapeDtypeStruct((rank, cols,...]
where the time goes in v6:
time: 95.1 us; the launch traced here: 95 us
  Pallas kernels  94.2 us (99%)
    pallas_call x1, Pallas kernels, body(): pl.pallas_call(whole_kernel, out_shape=(jax.ShapeDtypeStruct((rank, cols,...  92.1 us
    pallas_call x1, Pallas kernels, settle(): pl.pallas_call(settle_kernel, out_shape=(jax.ShapeDtypeStruct(result.shap...  2.09 us

profile of v6, /device:TPU:1, one launch (start us, length us, event | category | flops | bytes accessed | tf_op | source)
XLA Modules:
  0.0 95.0 jit_solution(15405439054342634620)
XLA Ops:
  0.6 92.1 %shard_map.203 = (f32[8,10,2,80]{3,2,1,0:T(2,128)}, bf16[2,2,320,320]{3,2,1,0:T(8,128)(2,1)}) custom-call(f32[2,8]{1,0:T(2,128)} %weight.1, f32[2,8]{1,0:T(2,128)} %level.1, f32[8,10,2,80]{3,2,1,0:T(2,128)} %bitcast.2, bf16[32,128]{1,0:T(8,128)(2,1)} %constant.41.clone.refs_1_, s32[2,640,640]{2,1,0:T(8,128)} %refs_2_.1, bf16[2,2,320,320]{3,2,1,0:T(8,128)(2,1)} %refs_3_.1, ...), custom_call_target="tpu_custom_call" | custom-call | tf_op jit(solution)/shard_map/pallas_call | solution.py:676
  92.7 2.1 %shard_map.204 = (f32[8,10,2,80]{3,2,1,0:T(2,128)}, bf16[2,2,320,320]{3,2,1,0:T(8,128)(2,1)}) custom-call(f32[8,10,2,80]{3,2,1,0:T(2,128)} %get-tuple-element.6.result, bf16[2,2,320,320]{3,2,1,0:T(8,128)(2,1)} %get-tuple-element.7.images), custom_call_target="tpu_custom_call" | custom-call | tf_op jit(solution)/shard_map/pallas_call | solution.py:609

commit v7 on v6

--- a/solution.py
+++ b/solution.py
@@ -268,14 +268,19 @@
             total += weights[d, t, pl.ds(r, 1)] * factors[r]
         return total.astype(BF)
 
+    def prepare(d, carry):
+        send_buf[t, d] = piece(d)
+        return carry
+
+    lax.fori_loop(0, nf, prepare, 0, unroll=8)
+
     def step(i, carry):
         d = lax.rem(frame + i, nf)
-        send_buf[t, d] = piece(d)
         remote(send_buf.at[t, d], recv_buf.at[t, frame], sems.at[0, t], sems.at[1, t], {"frame": d}).start()
         return carry
 
     lax.fori_loop(1, nf, step, 0)
-    recv_buf[t, frame] = piece(frame)
+    recv_buf[t, frame] = send_buf[t, frame]
 
 
 def wait_frames(buf, t, sem):

time: 95.1 us -> 95.4 us (level)
  no operation moved by 1% of the time
where the time goes in v7:
time: 95.4 us; the launch traced here: 95.2 us
  Pallas kernels  94.4 us (99%)
    pallas_call x1, Pallas kernels, body(): pl.pallas_call(whole_kernel, out_shape=(jax.ShapeDtypeStruct((rank, cols,...  92.3 us
    pallas_call x1, Pallas kernels, settle(): pl.pallas_call(settle_kernel, out_shape=(jax.ShapeDtypeStruct(result.shap...  2.09 us

profile of v7, /device:TPU:1, one launch (start us, length us, event | category | flops | bytes accessed | tf_op | source)
XLA Modules:
  0.0 95.2 jit_solution(15282833209957775142)
XLA Ops:
  0.6 92.3 %shard_map.203 = (f32[8,10,2,80]{3,2,1,0:T(2,128)}, bf16[2,2,320,320]{3,2,1,0:T(8,128)(2,1)}) custom-call(f32[2,8]{1,0:T(2,128)} %weight.1, f32[2,8]{1,0:T(2,128)} %level.1, f32[8,10,2,80]{3,2,1,0:T(2,128)} %bitcast.2, bf16[32,128]{1,0:T(8,128)(2,1)} %constant.41.clone.refs_1_, s32[2,640,640]{2,1,0:T(8,128)} %refs_2_.1, bf16[2,2,320,320]{3,2,1,0:T(8,128)(2,1)} %refs_3_.1, ...), custom_call_target="tpu_custom_call" | custom-call | tf_op jit(solution)/shard_map/pallas_call | solution.py:681
  93.0 2.1 %shard_map.204 = (f32[8,10,2,80]{3,2,1,0:T(2,128)}, bf16[2,2,320,320]{3,2,1,0:T(8,128)(2,1)}) custom-call(f32[8,10,2,80]{3,2,1,0:T(2,128)} %get-tuple-element.6.result, bf16[2,2,320,320]{3,2,1,0:T(8,128)(2,1)} %get-tuple-element.7.images), custom_call_target="tpu_custom_call" | custom-call | tf_op jit(solution)/shard_map/pallas_call | solution.py:614
